TPU v7x, 512 devices: a whole 4x4x16 slice. The times are simulated.
512 devices in a mesh: lat: 8 (over y, core), wave: 64 (over x, z).
Axes of the slice: x: 4, y: 4, z: 16, core: 2. Of those that a mesh axis runs over, the one named last changes fastest.
Arguments:
- grid_in: bfloat16 [1536, 64, 2560], P(('lat', 'wave')), may hold values from -6 to 6
- legendre: bfloat16 [640, 1536, 640], P('wave', 'lat'), may hold values from -0.15625 to 0.15625
- wave_order: int32 [640], replicated, may hold values from 0 to 639, as said below
- block_order: int32 [8], replicated, may hold values from 0 to 7, each once
- couple_div: float32 [32, 32], replicated, may hold values from -1 to 1
- couple_temp: float32 [32, 32], replicated, may hold values from -1 to 1
Outputs:
- spectral_out: bfloat16 [640, 640, 128], P('lat', 'wave')
- grid_out: bfloat16 [1536, 64, 2560], P(('lat', 'wave'))
Inputs may be any that keep to these rules, and one draw needn't show every extreme that they name: `wave_order`: slots 2i and 2i+1 hold wavenumbers m and 639 - m for some m; every wavenumber stands in exactly one slot. `block_order`: each block index stands once.
All inputs are finite; a program needn't handle non-finite values.
Results may differ from a plain program's by a relative error of at most 0.0085.
Values may be sent and summed in bfloat16 or wider, within the bound.
No kernel may reach another device: no remote copies, remote signals or barrier semaphores. Data moves between devices by JAX's collectives and lax.ppermute only.
A program may use at most 64 MiB of HBM per device.

v0:
```python
import math

import jax
import jax.numpy as jnp
from jax import lax
from jax.sharding import PartitionSpec as P


def trig_table(wave_order, lon_width):
    columns = jnp.arange(lon_width, dtype=jnp.int32)
    phase_turns = columns[:, None] * wave_order[None, :] % lon_width
    angles = phase_turns.astype(jnp.float32) * (2.0 * math.pi / lon_width)
    factor = 1.0 / math.sqrt(lon_width)
    return jnp.stack([jnp.cos(angles) * factor, -jnp.sin(angles) * factor], axis=-1).astype(
        jnp.bfloat16
    )


def implicit(values, degrees, couple_div, couple_temp, levels, top_degree):
    shaped = values.reshape(values.shape[0], values.shape[1], 2, 2, levels)
    div_part = shaped[:, :, :, 0, :]
    temp_part = shaped[:, :, :, 1, :]
    factor = (degrees * (degrees + 1)).astype(jnp.float32) / float(top_degree * top_degree)
    pulled = jnp.einsum("nscq,pq->nscp", temp_part, couple_div, precision=lax.Precision.HIGHEST)
    pushed = jnp.einsum("nscq,pq->nscp", div_part, couple_temp, precision=lax.Precision.HIGHEST)
    new_div = div_part - factor[:, :, None, None] * pulled
    new_temp = temp_part - pushed
    return jnp.stack([new_div, new_temp], axis=3).reshape(values.shape).astype(jnp.bfloat16)


def block_degrees(block_order, offset, amount, per_block):
    positions = offset + jnp.arange(amount, dtype=jnp.int32)
    block_ids = positions // per_block
    group_row = jnp.arange(block_order.shape[0], dtype=jnp.int32)
    chosen = jnp.sum(
        jnp.where(block_ids[:, None] == group_row[None, :], block_order[None, :], 0), axis=1
    )
    return chosen * per_block + positions % per_block


def body(grid_in, legendre, wave_order, block_order, couple_div, couple_temp):
    lat_rows, field_levels, lon_width = grid_in.shape
    total_slots = wave_order.shape[0]
    own_slots, band_rows, top_degree = legendre.shape
    levels = couple_div.shape[0]
    groups = lax.axis_size("lat")
    per_block = top_degree // groups
    columns = 2 * field_levels
    trig = trig_table(wave_order, lon_width)
    fourier = jnp.einsum("lfj,jsc->lscf", grid_in, trig, preferred_element_type=jnp.float32)
    fourier = fourier.astype(jnp.bfloat16).reshape(lat_rows, total_slots, columns)
    owned = lax.all_to_all(fourier, "wave", split_axis=1, concat_axis=0, tiled=True)
    own_waves = lax.dynamic_slice_in_dim(wave_order, lax.axis_index("wave") * own_slots, own_slots)
    my_offset = lax.axis_index("lat") * per_block
    degrees = block_degrees(block_order, jnp.int32(0), lax.axis_size("lat") * per_block, per_block)
    picked = jnp.take(legendre, degrees, axis=2)
    partial_value = jnp.einsum("sln,lsk->nsk", picked, owned, preferred_element_type=jnp.float32)
    keep_mask = degrees[:, None] >= own_waves[None, :]
    summed = lax.psum_scatter(
        jnp.where(keep_mask[:, :, None], partial_value, jnp.float32(0.0)),
        "lat",
        scatter_dimension=0,
        tiled=True,
    )
    degrees = block_degrees(block_order, my_offset, per_block, per_block)
    spectral_out = implicit(summed, degrees[:, None], couple_div, couple_temp, levels, top_degree)
    incoming = lax.all_gather(spectral_out, "lat", axis=0, tiled=True)
    degrees = block_degrees(block_order, jnp.int32(0), incoming.shape[0], per_block)
    picked = jnp.take(legendre, degrees, axis=2)
    returned = jnp.einsum("sln,nsk->lsk", picked, incoming, preferred_element_type=jnp.float32)
    returned = returned.astype(jnp.bfloat16)
    lat_back = lax.all_to_all(returned, "wave", split_axis=0, concat_axis=1, tiled=True)
    weight = jnp.where(wave_order == 0, 1.0, 2.0).astype(jnp.bfloat16)
    weighted = trig * weight[None, :, None]
    shaped_back = lat_back.reshape(lat_rows, total_slots, 2, field_levels)
    grid_out = jnp.einsum(
        "lscf,jsc->lfj", shaped_back, weighted, preferred_element_type=jnp.float32
    )
    return (spectral_out, grid_out.astype(jnp.bfloat16))


def solution(mesh):
    placed = (P(("lat", "wave"), None, None), P("wave", "lat", None), P(), P(), P(), P())
    return jax.shard_map(
        body,
        mesh=mesh,
        in_specs=placed,
        out_specs=(P("lat", "wave", None), P(("lat", "wave"), None, None)),
        check_vma=False,
    )
```

profile of v0, /device:TPU:6, one launch (start us, length us, event | category | flops | bytes accessed | tf_op | source)
XLA Modules:
  0.0 262.6 jit_solution(14977282368567734306)
XLA Ops:
  7.2 28.4 %multiply_convert_fusion.1 = (bf16[2560,640,1]{1,0,2:T(8,128)(2,1)S(1)}, bf16[2560,640,1]{1,0,2:T(8,128)(2,1)S(1)}) fusion(s32[640]{0:T(1024)} %param.10), kind=kLoop, calls=%fused_computation.11 | loop fusion | flops 22937600 | bytes 6556160 | tf_op jit(solution)/shard_map/convert.4
  35.6 1.4 fusion.21
  37.3 1.4 copy-done.2
  39.5 2.1 copy.55
  41.6 19.0 %all-to-all-start = ((bf16[3,640,128]{2,0,1:T(4,128)(2,1)}), bf16[3,640,128]{2,0,1:T(4,128)(2,1)}, u32[]{:S(2)}, u32[]{:S(2)}) async-start(bf16[3,640,128]{2,0,1:T(4,128)(2,1)} %copy.55), calls=%async_computation | async-start | bytes 1310720 | tf_op jit(solution)/shard_map/all_to_all | solution.py:52
  60.9 8.1 %copy.58 = bf16[10,192,640]{1,0,2:T(8,128)(2,1)} copy(bf16[10,192,640]{2,1,0:T(8,128)(2,1)S(1)} %copy-done.3) | data formatting | bytes 4915200 | tf_op args[1]
  69.2 7.2 %gather_fusion = bf16[640,10,192]{2,1,0:T(8,128)(2,1)} fusion(bf16[10,192,640]{1,0,2:T(8,128)(2,1)} %copy.58, s32[1024]{0:T(1024)S(1)} %pad_clamp_fusion), kind=kCustom, calls=%fused_computation.clone | custom fusion | bytes 4917760 | tf_op jit(solution)/shard_map/jit(_take)/gather | solution.py:56
  76.4 6.9 %select_bitcast_fusion = bf16[10,192,640]{1,0,2:T(8,128)(2,1)} fusion(bf16[640,10,192]{2,1,0:T(8,128)(2,1)} %gather_fusion, pred[640]{0:T(1024)(128)(4,1)S(1)} %compare_and_fusion), kind=kLoop, calls=%fused_computation.16 | loop fusion | flops 1228800 | bytes 4915840 | tf_op jit(solution)/shard_map/jit(_take)/select_n | solution.py:56
  83.3 6.0 %copy.59 = bf16[10,192,640]{2,1,0:T(8,128)(2,1)S(1)} copy(bf16[10,192,640]{1,0,2:T(8,128)(2,1)} %select_bitcast_fusion) | data formatting | bytes 4915200 | tf_op jit(solution)/shard_map/jit(_take)/select_n | solution.py:56
  89.4 8.4 %all-to-all-done = bf16[3,640,128]{2,0,1:T(4,128)(2,1)} async-done(((bf16[3,640,128]{2,0,1:T(4,128)(2,1)}), bf16[3,640,128]{2,0,1:T(4,128)(2,1)}, u32[]{:S(2)}, u32[]{:S(2)}) %all-to-all-start) | async-done | bytes 491552 | tf_op jit(solution)/shard_map/all_to_all | solution.py:52
  99.0 1.3 copy.57
  100.2 2.1 all_to_all.27
  102.3 3.4 %bitcast_select_fusion = f32[640,10,128]{0,2,1:T(8,128)} fusion(bf16[192,10,128]{2,0,1:T(8,128)(2,1)} %all_to_all.27, bf16[10,192,640]{2,1,0:T(8,128)(2,1)S(1)} %copy.59, pred[640,10]{0,1:T(8,128)(4,1)S(1)} %broadcast_compare_fusion), kind=kOutput, calls=%fused_computation.19 | convolution fusion | flops 315392000 | bytes 6232320 | tf_op jit(solution)/shard_map/sln,lsk->nsk/dot_general | solution.py:57
  105.8 4.6 %copy.79 = f32[640,1280]{1,0:T(8,128)} copy(f32[640,1280]{0,1:T(8,128)} %bitcast.84) | data formatting | bytes 6553600
  110.6 36.1 %reduce-scatter.4.cloned.1.call-done = f32[80,1280]{1,0:T(8,128)} async-done(((f32[640,1280]{1,0:T(8,128)}), f32[80,1280]{1,0:T(8,128)}) %reduce-scatter.4.cloned.1.call-update) | async-done | bytes 409616
  146.6 2.1 copy.80
  148.7 1.5 fusion.27
  150.2 1.5 fusion.28
  152.5 1.8 copy.69
  154.4 31.1 %all-gather.2.cloned.1.call-done = bf16[640,10,128]{2,0,1:T(8,128)(2,1)} async-done(((bf16[80,10,128]{2,0,1:T(8,128)(2,1)}), bf16[640,10,128]{2,0,1:T(8,128)(2,1)}) %all-gather.2.cloned.1.call-update) | async-done | bytes 1638416 | tf_op jit(solution)/shard_map/all_gather | solution.py:67
  185.5 2.2 fusion.20
  188.9 15.9 %all-to-all-start.1 = ((bf16[192,10,128]{2,1,0:T(8,128)(2,1)}), bf16[192,10,128]{2,1,0:T(8,128)(2,1)S(1)}, u32[]{:S(2)}, u32[]{:S(2)}) async-start(bf16[192,10,128]{2,1,0:T(8,128)(2,1)} %copy.65), calls=%async_computation.1 | async-start | bytes 1572864 | tf_op jit(solution)/shard_map/all_to_all | solution.py:72
  204.9 43.2 %all-to-all-done.1 = bf16[192,10,128]{2,1,0:T(8,128)(2,1)S(1)} async-done(((bf16[192,10,128]{2,1,0:T(8,128)(2,1)}), bf16[192,10,128]{2,1,0:T(8,128)(2,1)S(1)}, u32[]{:S(2)}, u32[]{:S(2)}) %all-to-all-start.1) | async-done | bytes 491552 | tf_op jit(solution)/shard_map/all_to_all | solution.py:72
  249.0 6.8 %fusion.13 = bf16[3,64,2560]{2,1,0:T(8,128)(2,1)} fusion(bf16[2560,640,1]{1,0,2:T(8,128)(2,1)} %copy-done.2, bf16[2560,640,1]{1,0,2:T(8,128)(2,1)} %copy-done.1, bf16[640]{0:T(1024)(128)(2,1)S(1)} %select_convert_fusion, bf16[3,640,2,64]{3,2,0,1:T(2,128)(2,1)S(1)} %reshape.197), kind=kOutput, calls=%fused_computation.18 | convolution fusion | flops 1265336320 | bytes 8029440 | tf_op jit(solution)/shard_map/lscf,jsc->lfj/dot_general | solution.py:76
  (37 shorter events, 5.9 us)
Async XLA Ops:
  7.2 28.4 %copy-start = (bf16[3,64,2560]{2,1,0:T(8,128)(2,1)S(1)}, bf16[3,64,2560]{2,1,0:T(8,128)(2,1)}, u32[]{:S(2)}) copy-start(bf16[3,64,2560]{2,1,0:T(8,128)(2,1)} %param.8) | copy-start | bytes 2949124
  35.6 1.7 copy-start.1
  35.6 3.1 %copy-start.2 = (bf16[2560,640,1]{1,0,2:T(8,128)(2,1)}, bf16[2560,640,1]{1,0,2:T(8,128)(2,1)S(1)}, u32[]{:S(2)}) copy-start(bf16[2560,640,1]{1,0,2:T(8,128)(2,1)S(1)} %get-tuple-element.14) | copy-start | bytes 9830404
  35.6 25.2 %copy-start.6 = (s32[640]{0:T(1024)S(1)}, s32[640]{0:T(1024)}, u32[]{:S(2)}) copy-start(s32[640]{0:T(1024)} %param.10) | copy-start | bytes 7684
  35.6 25.3 %copy-start.3 = (bf16[10,192,640]{2,1,0:T(8,128)(2,1)S(1)}, bf16[10,192,640]{2,1,0:T(8,128)(2,1)}, u32[]{:S(2)}) copy-start(bf16[10,192,640]{2,1,0:T(8,128)(2,1)} %param.9) | copy-start | bytes 7372804
  39.5 29.5 %copy-start.7 = (s32[8]{0:T(128)S(1)}, s32[8]{0:T(128)}, u32[]{:S(2)}) copy-start(s32[8]{0:T(128)} %param.11) | copy-start | bytes 100
  41.6 56.1 %all-to-all-start = ((bf16[3,640,128]{2,0,1:T(4,128)(2,1)}), bf16[3,640,128]{2,0,1:T(4,128)(2,1)}, u32[]{:S(2)}, u32[]{:S(2)}) async-start(bf16[3,640,128]{2,0,1:T(4,128)(2,1)} %copy.55), calls=%async_computation | async-start | bytes 1310720 | tf_op jit(solution)/shard_map/all_to_all | solution.py:52
  60.6 86.0 %reduce-scatter.4.cloned.1.call-start = ((), (), s32[]{:S(2)}) async-start(), calls=%async_computation.4 | async-start | bytes 3686400
  105.8 42.9 %copy-start.4 = (f32[32,32]{1,0:T(8,128)S(1)}, f32[32,32]{1,0:T(8,128)}, u32[]{:S(2)}) copy-start(f32[32,32]{1,0:T(8,128)} %param.13) | copy-start | bytes 12292
  105.8 44.4 %copy-start.5 = (f32[32,32]{1,0:T(8,128)S(1)}, f32[32,32]{1,0:T(8,128)}, u32[]{:S(2)}) copy-start(f32[32,32]{1,0:T(8,128)} %param.12) | copy-start | bytes 12292
  110.4 75.1 %all-gather.2.cloned.1.call-start = ((), (), s32[]{:S(2)}) async-start(), calls=%async_computation.3 | async-start | bytes 1843200 | tf_op jit(solution)/shard_map/all_gather | solution.py:67
  188.9 59.2 %all-to-all-start.1 = ((bf16[192,10,128]{2,1,0:T(8,128)(2,1)}), bf16[192,10,128]{2,1,0:T(8,128)(2,1)S(1)}, u32[]{:S(2)}, u32[]{:S(2)}) async-start(bf16[192,10,128]{2,1,0:T(8,128)(2,1)} %copy.65), calls=%async_computation.1 | async-start | bytes 1572864 | tf_op jit(solution)/shard_map/all_to_all | solution.py:72
Sparse Core Ops, SparseCore 0:
  110.5 36.0 reduce-scatter.3
  154.5 30.9 all-gather.1
where the time goes:
time: 263 us
  waiting for transfers between devices  119 us (45%)
  local copies, waits for them, and re-layouts  41.8 us (16%)
  other arithmetic  35.7 us (14%)
  starting transfers between devices  35.1 us (13%)
  matrix products  16.8 us (6%)
  between operations  14.2 us (5%)
    all_to_all x1, waiting for transfers between devices, body(): lax.all_to_all(returned, 'wave', split_axis=0, concat_axis=1, tiled=True)  43.2 us
    unnamed x3, waiting for transfers between devices  36.1 us
    all_gather x1, waiting for transfers between devices, body(): incoming = lax.all_gather(spectral_out, 'lat', axis=0, tiled=True)  31.1 us
    another operation x1, other arithmetic  28.4 us
    all_to_all x1, starting transfers between devices, body(): lax.all_to_all(fourier, 'wave', split_axis=1, concat_axis=0, tiled=True)  19 us
    unnamed x20, local copies, waits for them, and re-layouts  18.2 us
    all_to_all x1, starting transfers between devices, body(): lax.all_to_all(returned, 'wave', split_axis=0, concat_axis=1, tiled=True)  15.9 us
    all_to_all x1, waiting for transfers between devices, body(): lax.all_to_all(fourier, 'wave', split_axis=1, concat_axis=0, tiled=True)  8.39 us
  transfers between devices with their start and end apart: 4, of which 4 were waited for; matrix products, arithmetic and copies ran while one was open for 11% of the time, Pallas kernels for 0%

commit v1 on v0

v1 whole, which is shorter than its diff:
```python
import functools
import math

import jax
import jax.numpy as jnp
from jax import lax
from jax.experimental import pallas as pl
from jax.experimental.pallas import tpu as pltpu
from jax.sharding import PartitionSpec as P

F32 = jnp.float32
BF16 = jnp.bfloat16
NLON = 2560
WAVES = 64
GROUPS = 8
SLOTS = 10
ROWS = 3
FIELDS = 64
K = 128
TOP = 640
BAND = 192
CHUNK = 32
UNIT = 16
UNITS = TOP // UNIT
PAIR_ROWS = TOP + UNIT
PACKED = 3328
SHARE = PACKED // GROUPS
VMEM_LIMIT = 56 * 1024 * 1024


def params():
    return pltpu.CompilerParams(
        dimension_semantics=("arbitrary",), vmem_limit_bytes=VMEM_LIMIT
    )


def cos_sin(phase):
    quarter = (
        (phase >= 320.0).astype(F32)
        + (phase >= 960.0).astype(F32)
        + (phase >= 1600.0).astype(F32)
        + (phase >= 2240.0).astype(F32)
    )
    x = (phase - 640.0 * quarter) * (2.0 * math.pi / NLON)
    y = x * x
    s = x * (
        1.0 + y * (-1.0 / 6 + y * (1.0 / 120 + y * (-1.0 / 5040 + y * (1.0 / 362880))))
    )
    c = 1.0 + y * (
        -0.5 + y * (1.0 / 24 + y * (-1.0 / 720 + y * (1.0 / 40320 + y * (-1.0 / 3628800))))
    )
    odd = (quarter == 1.0) | (quarter == 3.0)
    cos = jnp.where(odd, s, c)
    sin = jnp.where(odd, c, s)
    cos = jnp.where((quarter == 1.0) | (quarter == 2.0), -cos, cos)
    sin = jnp.where((quarter == 2.0) | (quarter == 3.0), -sin, sin)
    return cos, sin


def phase_of(product):
    return product - NLON * jnp.floor((product + 0.5) * (1.0 / NLON))


def forward_kernel(waves_ref, grid_ref, table_ref, send_ref, rows):
    step = pl.program_id(0)
    waves = waves_ref[...]
    lanes = lax.broadcasted_iota(jnp.int32, waves.shape, 1).astype(F32)
    near_c, near_s = cos_sin(phase_of(waves * lanes))
    far_c, far_s = cos_sin(phase_of(waves * (lanes * 128.0)))
    factor = 1.0 / math.sqrt(NLON)
    far_c = far_c * factor
    far_s = far_s * factor
    for a in range(NLON // 128):
        ca = far_c[:, a : a + 1]
        sa = far_s[:, a : a + 1]
        at = slice(a * 128, (a + 1) * 128)
        table_ref[0, :, at] = (ca * near_c - sa * near_s).astype(BF16)
        table_ref[1, :, at] = (-(sa * near_c) - ca * near_s).astype(BF16)
    table = table_ref[...].reshape(256, NLON)
    made = lax.dot_general(
        table, grid_ref[...], (((1,), (1,)), ((), ())), preferred_element_type=F32
    )
    for li in range(ROWS):
        at = slice(li * FIELDS, (li + 1) * FIELDS)
        both = jnp.concatenate([made[:128, at], made[128:, at]], axis=1)
        for q in range(2):
            row = (2 * step + q) * ROWS + li
            rows[pl.ds(row, WAVES, stride=CHUNK), :] = both[q * 64 : (q + 1) * 64]

    @pl.when(step == 4)
    def _():
        for row in range(SLOTS * ROWS, CHUNK):
            rows[pl.ds(row, WAVES, stride=CHUNK), :] = jnp.zeros((WAVES, K), F32)
        send_ref[...] = rows[...].astype(BF16)


def forward(waves, grid):
    return pl.pallas_call(
        forward_kernel,
        grid=(5,),
        in_specs=[
            pl.BlockSpec((128, 128), lambda i: (i, 0)),
            pl.BlockSpec((ROWS * FIELDS, NLON), lambda i: (0, 0)),
        ],
        out_specs=[
            pl.BlockSpec((2, 128, NLON), lambda i: (0, i, 0)),
            pl.BlockSpec((WAVES * CHUNK, K), lambda i: (0, 0)),
        ],
        out_shape=[
            jax.ShapeDtypeStruct((2, TOP, NLON), BF16),
            jax.ShapeDtypeStruct((WAVES * CHUNK, K), BF16),
        ],
        scratch_shapes=[pltpu.VMEM((WAVES * CHUNK, K), F32)],
        compiler_params=params(),
        cost_estimate=pl.CostEstimate(
            flops=2 * 192 * 2560 * 1280, bytes_accessed=9000000, transcendentals=0
        ),
        name="forward_rows",
    )(waves, grid)


def basis_kernel(own_ref, leg_ref, straight_ref, turned_ref, rows):
    wave = own_ref[pl.program_id(0)]
    for b in range(TOP // 128):
        at = slice(b * 128, (b + 1) * 128)
        rows[b] = leg_ref[0, :, at].astype(F32)
        for li in range(ROWS):
            straight_ref[0, li * WAVES : (li + 1) * WAVES, at] = rows[
                b, pl.ds(li, WAVES, stride=ROWS), :
            ].astype(BF16)
    turned = straight_ref[0].astype(F32).T
    degree = lax.broadcasted_iota(jnp.int32, turned.shape, 0)
    turned_ref[0] = jnp.where(degree >= wave, turned, 0.0).astype(BF16)


def basis(own, legendre):
    return pl.pallas_call(
        basis_kernel,
        grid=(SLOTS,),
        in_specs=[
            pl.BlockSpec(memory_space=pltpu.SMEM),
            pl.BlockSpec((1, BAND, TOP), lambda i: (i, 0, 0)),
        ],
        out_specs=[
            pl.BlockSpec((1, BAND, TOP), lambda i: (i, 0, 0)),
            pl.BlockSpec((1, TOP, BAND), lambda i: (i, 0, 0)),
        ],
        out_shape=[
            jax.ShapeDtypeStruct((SLOTS, BAND, TOP), BF16),
            jax.ShapeDtypeStruct((SLOTS, TOP, BAND), BF16),
        ],
        scratch_shapes=[pltpu.VMEM((TOP // 128, BAND, 128), F32)],
        compiler_params=params(),
        cost_estimate=pl.CostEstimate(
            flops=0, bytes_accessed=30000000, transcendentals=0
        ),
        name="basis_rows",
    )(own, legendre)


def partial_kernel(own_ref, turned_ref, got_ref, packed_ref, rows, tail):
    step = pl.program_id(0)

    @pl.when(step == 0)
    def _():
        rows[...] = got_ref[...].astype(F32)
        packed_ref[5 * PAIR_ROWS :, :] = jnp.zeros((PACKED - 5 * PAIR_ROWS, K), BF16)
        tail[TOP:, :] = jnp.zeros((TOP, K), F32)

    def product(q):
        slot = 2 * step + q
        values = jnp.concatenate(
            [
                rows[pl.ds(slot * ROWS + li, WAVES, stride=CHUNK), :]
                for li in range(ROWS)
            ],
            axis=0,
        ).astype(BF16)
        return jnp.dot(turned_ref[q], values, preferred_element_type=F32)

    unit = own_ref[2 * step] // UNIT
    tail[:TOP, :] = product(1)
    first = product(0)
    start = pl.multiple_of((UNITS - 1 - unit) * UNIT, UNIT)
    second = tail[pl.ds(start, PAIR_ROWS), :]
    first = jnp.concatenate([jnp.zeros((UNIT, K), F32), first], axis=0)
    row = lax.broadcasted_iota(jnp.int32, (PAIR_ROWS, K), 0)
    joined = jnp.where(row >= (unit + 1) * UNIT, first, second)
    at = pl.multiple_of(step * PAIR_ROWS, UNIT)
    packed_ref[pl.ds(at, PAIR_ROWS), :] = joined.astype(BF16)


def partial_sums(own, turned, got):
    return pl.pallas_call(
        partial_kernel,
        grid=(5,),
        in_specs=[
            pl.BlockSpec(memory_space=pltpu.SMEM),
            pl.BlockSpec((2, TOP, BAND), lambda i: (i, 0, 0)),
            pl.BlockSpec((WAVES * CHUNK, K), lambda i: (0, 0)),
        ],
        out_specs=pl.BlockSpec((PACKED, K), lambda i: (0, 0)),
        out_shape=jax.ShapeDtypeStruct((PACKED, K), BF16),
        scratch_shapes=[
            pltpu.VMEM((WAVES * CHUNK, K), F32),
            pltpu.VMEM((2 * TOP, K), F32),
        ],
        compiler_params=params(),
        cost_estimate=pl.CostEstimate(
            flops=2 * 10 * 192 * 640 * 128, bytes_accessed=5000000, transcendentals=0
        ),
        name="partial_sums",
    )(own, turned, got)


def couple_kernel(parts_ref, factor_ref, couple_ref, out_ref):
    total = parts_ref[0].astype(F32)
    for g in range(1, GROUPS):
        total = total + parts_ref[g].astype(F32)
    pulled = jnp.dot(
        total,
        couple_ref[...],
        preferred_element_type=F32,
        precision=lax.Precision.HIGHEST,
    )
    out_ref[...] = (total - factor_ref[...] * pulled).astype(BF16)


def couple(parts, factor, matrix):
    return pl.pallas_call(
        couple_kernel,
        out_shape=jax.ShapeDtypeStruct((SHARE, K), BF16),
        compiler_params=pltpu.CompilerParams(vmem_limit_bytes=VMEM_LIMIT),
        cost_estimate=pl.CostEstimate(
            flops=2 * 416 * 128 * 128 * 6, bytes_accessed=1200000, transcendentals=0
        ),
        name="couple_levels",
    )(parts, factor, matrix)


def inverse_kernel(own_ref, block_ref, straight_ref, all_ref, out_ref, send_ref, held, one, rows):
    step = pl.program_id(0)

    @pl.when(step == 0)
    def _():
        held[:TOP, :] = jnp.zeros((TOP, K), BF16)
        held[TOP:, :] = all_ref[...]

    unit = own_ref[2 * step] // UNIT
    row = lax.broadcasted_iota(jnp.int32, (TOP, K), 0)
    begin = block_ref[0] * (TOP // GROUPS)
    for q in range(2):
        if q == 0:
            start = TOP + step * PAIR_ROWS + UNIT
            least = unit * UNIT
        else:
            least = (UNITS - 1 - unit) * UNIT
            start = TOP + step * PAIR_ROWS - least
        start = pl.multiple_of(start, UNIT)
        values = held[pl.ds(start, TOP), :].astype(F32)
        one[q] = jnp.where(row >= least, values, 0.0).astype(BF16)
        out_ref[q] = one[q, pl.ds(pl.multiple_of(begin, UNIT), TOP // GROUPS), :]
        back = jnp.dot(straight_ref[q], one[q], preferred_element_type=F32)
        weight = jnp.where(own_ref[2 * step + q] == 0, 1.0, 2.0)
        back = back * weight
        for li in range(ROWS):
            at = (2 * step + q) * ROWS + li
            rows[pl.ds(at, WAVES, stride=CHUNK), :] = back[li * WAVES : (li + 1) * WAVES]

    @pl.when(step == 4)
    def _():
        for at in range(SLOTS * ROWS, CHUNK):
            rows[pl.ds(at, WAVES, stride=CHUNK), :] = jnp.zeros((WAVES, K), F32)
        send_ref[...] = rows[...].astype(BF16)


def inverse(own, block, straight, everything):
    return pl.pallas_call(
        inverse_kernel,
        grid=(5,),
        in_specs=[
            pl.BlockSpec(memory_space=pltpu.SMEM),
            pl.BlockSpec(memory_space=pltpu.SMEM),
            pl.BlockSpec((2, BAND, TOP), lambda i: (i, 0, 0)),
            pl.BlockSpec((PACKED, K), lambda i: (0, 0)),
        ],
        out_specs=[
            pl.BlockSpec((2, TOP // GROUPS, K), lambda i: (i, 0, 0)),
            pl.BlockSpec((WAVES * CHUNK, K), lambda i: (0, 0)),
        ],
        out_shape=[
            jax.ShapeDtypeStruct((SLOTS, TOP // GROUPS, K), BF16),
            jax.ShapeDtypeStruct((WAVES * CHUNK, K), BF16),
        ],
        scratch_shapes=[
            pltpu.VMEM((TOP + PACKED, K), BF16),
            pltpu.VMEM((2, TOP, K), BF16),
            pltpu.VMEM((WAVES * CHUNK, K), F32),
        ],
        compiler_params=params(),
        cost_estimate=pl.CostEstimate(
            flops=2 * 10 * 192 * 640 * 128, bytes_accessed=5000000, transcendentals=0
        ),
        name="inverse_sums",
    )(own, block, straight, everything)


def finish_kernel(got_ref, table_ref, out_ref, rows, left):
    @pl.when(pl.program_id(0) == 0)
    def _():
        rows[...] = got_ref[...].astype(F32)
        for li in range(ROWS):
            values = jnp.concatenate(
                [
                    rows[pl.ds(slot * ROWS + li, WAVES, stride=CHUNK), :]
                    for slot in range(SLOTS)
                ],
                axis=0,
            )
            turned = values.T.astype(BF16)
            at = slice(li * FIELDS, (li + 1) * FIELDS)
            left[at, :TOP] = turned[:FIELDS]
            left[at, TOP:] = turned[FIELDS:]

    table = table_ref[...].reshape(2 * TOP, table_ref.shape[2])
    out_ref[...] = jnp.dot(left[...], table, preferred_element_type=F32).astype(BF16)


def finish(got, table):
    block = 512
    return pl.pallas_call(
        finish_kernel,
        grid=(NLON // block,),
        in_specs=[
            pl.BlockSpec((WAVES * CHUNK, K), lambda i: (0, 0)),
            pl.BlockSpec((2, TOP, block), lambda i: (0, 0, i)),
        ],
        out_specs=pl.BlockSpec((ROWS * FIELDS, block), lambda i: (0, i)),
        out_shape=jax.ShapeDtypeStruct((ROWS * FIELDS, NLON), BF16),
        scratch_shapes=[
            pltpu.VMEM((WAVES * CHUNK, K), F32),
            pltpu.VMEM((ROWS * FIELDS, 2 * TOP), BF16),
        ],
        compiler_params=params(),
        cost_estimate=pl.CostEstimate(
            flops=2 * 192 * 2560 * 1280, bytes_accessed=9000000, transcendentals=0
        ),
        name="finish_rows",
    )(got, table)


def coupling_matrix(couple_div, couple_temp):
    zero = jnp.zeros_like(couple_div)
    one = jnp.block([[zero, couple_temp.T], [couple_div.T, zero]])
    none = jnp.zeros_like(one)
    return jnp.block([[one, none], [none, one]])


def packed_factor(own, offset):
    position = offset + lax.broadcasted_iota(jnp.int32, (SHARE, K), 0)
    column = lax.broadcasted_iota(jnp.int32, (SHARE, K), 1)
    pair = position // PAIR_ROWS
    inside = position - pair * PAIR_ROWS
    unit = jnp.zeros((SHARE, K), jnp.int32)
    for i in range(SLOTS // 2):
        unit = jnp.where(pair == i, own[2 * i] // UNIT, unit)
    degree = jnp.where(
        inside >= (unit + 1) * UNIT, inside - UNIT, inside + (UNITS - 1 - unit) * UNIT
    )
    factor = (degree * (degree + 1)).astype(F32) / float(TOP * TOP)
    return jnp.where(column % (K // 2) < K // 4, factor, 1.0)


def body(grid_in, legendre, wave_order, block_order, couple_div, couple_temp):
    lat = lax.axis_index("lat")
    wave = lax.axis_index("wave")
    own = lax.dynamic_slice_in_dim(wave_order, wave * SLOTS, SLOTS)
    block = lax.dynamic_slice_in_dim(block_order, lat, 1)
    waves = wave_order.reshape(WAVES, SLOTS).T.reshape(TOP, 1).astype(F32)
    waves = jnp.broadcast_to(waves, (TOP, 128))
    table, send = forward(waves, grid_in.reshape(ROWS * FIELDS, NLON))
    swap = functools.partial(lax.all_to_all, split_axis=0, concat_axis=0, tiled=True)
    got = swap(send.reshape(WAVES, CHUNK, K), "wave")
    straight, turned = basis(own, legendre)
    matrix = coupling_matrix(couple_div, couple_temp)
    factor = packed_factor(own, lat * SHARE)
    packed = partial_sums(own, turned, got.reshape(WAVES * CHUNK, K))
    parts = swap(packed.reshape(GROUPS, SHARE, K), "lat")
    spectral = couple(parts, factor, matrix)
    everything = lax.all_gather(spectral, "lat", axis=0, tiled=True)
    spectral_out, send = inverse(own, block, straight, everything)
    got = swap(send.reshape(WAVES, CHUNK, K), "wave")
    grid_out = finish(got.reshape(WAVES * CHUNK, K), table)
    return spectral_out.transpose(1, 0, 2), grid_out.reshape(ROWS, FIELDS, NLON)


def solution(mesh):
    placed = (P(("lat", "wave"), None, None), P("wave", "lat", None), P(), P(), P(), P())
    return jax.shard_map(
        body,
        mesh=mesh,
        in_specs=placed,
        out_specs=(P("lat", "wave", None), P(("lat", "wave"), None, None)),
        check_vma=False,
    )
```

time: 263 us -> 160 us (0.61)
  waiting for transfers between devices: 119 us -> 20.8 us
  blocking collectives: 0 us -> 54 us
  Pallas kernels: 0 us -> 39.8 us
  local copies, waits for them, and re-layouts: 41.8 us -> 5.12 us
  other arithmetic: 35.7 us -> 2.5 us
  matrix products: 16.8 us -> 0 us
  starting transfers between devices: 35.1 us -> 23.3 us
    pallas_call x0 -> x6, Pallas kernels: none -> 39.8 us  [the longest x1 9.97 us: forward(): pl.pallas_call(forward_kernel, grid=(5,), in_specs=[pl.BlockSpec((128, 12...]
    all_to_all x0 -> x1, blocking collectives: none -> 39.2 us  [body(): got = swap(send.reshape(WAVES, CHUNK, K), 'wave')]
    unnamed x3 -> x0, waiting for transfers between devices: 36.1 us -> none
    all_gather x1 -> x0, waiting for transfers between devices: 31.1 us -> none  [body(): incoming = lax.all_gather(spectral_out, 'lat', axis=0, tiled=True)]
    all_to_all x2, waiting for transfers between devices: 51.6 us -> 20.8 us  [the longest x1 12 us: body(): parts = swap(packed.reshape(GROUPS, SHARE, K), 'lat')]
    another operation x2 -> x0, other arithmetic: 28.5 us -> none
    dot_general x6 -> x0, matrix products: 16.8 us -> none  [the longest x1 6.75 us: body(): jnp.einsum('lscf,jsc->lfj', shaped_back, weighted, preferred_element_type...]
    unnamed x20 -> x14, local copies, waits for them, and re-layouts: 18.2 us -> 1.88 us
  transfers between devices with their start and end apart: 4 -> 2, of which waited for: 4 -> 2; matrix products, arithmetic and copies ran while one was open for 11% -> 3% of each run, Pallas kernels for 0% -> 5%
where the time goes in v1:
time: 160 us; the launch traced here: 159 us
  blocking collectives  54 us (34%)
  Pallas kernels  39.8 us (25%)
  starting transfers between devices  23.3 us (15%)
  waiting for transfers between devices  20.8 us (13%)
  between operations  13.3 us (8%)
  local copies, waits for them, and re-layouts  5.12 us (3%)
  other arithmetic  2.5 us (2%)
    all_to_all x1, blocking collectives, body(): got = swap(send.reshape(WAVES, CHUNK, K), 'wave')  39.2 us
    all_to_all x1, starting transfers between devices, body(): got = swap(send.reshape(WAVES, CHUNK, K), 'wave')  18.8 us
    all_gather x1, blocking collectives, body(): everything = lax.all_gather(spectral, 'lat', axis=0, tiled=True)  14.7 us
    all_to_all x1, waiting for transfers between devices, body(): parts = swap(packed.reshape(GROUPS, SHARE, K), 'lat')  12 us
    pallas_call x1, Pallas kernels, forward(): pl.pallas_call(forward_kernel, grid=(5,), in_specs=[pl.BlockSpec((128, 12...  9.97 us
    all_to_all x1, waiting for transfers between devices, body(): got = swap(send.reshape(WAVES, CHUNK, K), 'wave')  8.79 us
    pallas_call x1, Pallas kernels, basis(): pl.pallas_call(basis_kernel, grid=(SLOTS,), in_specs=[pl.BlockSpec(memory...  8.06 us
    pallas_call x1, Pallas kernels, finish(): pl.pallas_call(finish_kernel, grid=(NLON // block,), in_specs=[pl.BlockSp...  6.97 us
  transfers between devices with their start and end apart: 2, of which 2 were waited for; matrix products, arithmetic and copies ran while one was open for 3% of the time, Pallas kernels for 5%

profile of v1, /device:TPU:6, one launch (start us, length us, event | category | flops | bytes accessed | tf_op | source)
XLA Modules:
  0.0 158.8 jit_solution(13841274539006527293)
XLA Ops:
  0.6 0.7 convert_element_type.20
  1.3 0.1 convert_element_type.21
  1.5 0.1 copy.10
  1.6 0.9 broadcast_in_dim.27.waves_ref
  2.5 10.0 %forward_rows.1 = (bf16[2,640,2560]{2,1,0:T(8,128)(2,1)}, bf16[2048,128]{1,0:T(8,128)(2,1)}) custom-call(f32[640,128]{1,0:T(8,128)} %broadcast_in_dim.27.waves_ref, bf16[192,2560]{1,0:T(8,128)(2,1)} %bitcast.25), custom_call_target="tpu_custom_call" | custom-call | flops 1258291200 | bytes 9000000 | tf_op jit(solution)/shard_map/forward_rows/pallas_call | solution.py:98
  12.5 18.8 %all-to-all-start = ((bf16[64,32,128]{2,1,0:T(8,128)(2,1)}), bf16[64,32,128]{2,1,0:T(8,128)(2,1)S(1)}, u32[]{:S(2)}, u32[]{:S(2)}) async-start(bf16[64,32,128]{2,1,0:T(8,128)(2,1)} %bitcast.20), calls=%async_computation | async-start | bytes 1048576 | tf_op jit(solution)/shard_map/all_to_all | solution.py:383
  31.3 0.8 dynamic_slice.6.own_ref
  32.1 0.6 fusion.10
  45.3 8.1 %basis_rows.1 = (bf16[10,192,640]{2,1,0:T(8,128)(2,1)}, bf16[10,640,192]{2,1,0:T(8,128)(2,1)}) custom-call(s32[10]{0:T(128)} %copy-done.2, bf16[10,192,640]{2,1,0:T(8,128)(2,1)} %leg_ref.1), custom_call_target="tpu_custom_call" | custom-call | bytes 30000000 | tf_op jit(solution)/shard_map/basis_rows/pallas_call | solution.py:137
  53.5 0.6 dynamic_slice.7.block_ref
  54.2 8.8 %all-to-all-done = bf16[64,32,128]{2,1,0:T(8,128)(2,1)S(1)} async-done(((bf16[64,32,128]{2,1,0:T(8,128)(2,1)}), bf16[64,32,128]{2,1,0:T(8,128)(2,1)S(1)}, u32[]{:S(2)}, u32[]{:S(2)}) %all-to-all-start) | async-done | bytes 524320 | tf_op jit(solution)/shard_map/all_to_all | solution.py:383
  63.0 0.8 copy-done.1
  63.8 5.8 %partial_sums.1 = bf16[3328,128]{1,0:T(8,128)(2,1)} custom-call(s32[10]{0:T(128)} %copy-done.2, bf16[10,640,192]{2,1,0:T(8,128)(2,1)} %get-tuple-element.9.turned_ref, bf16[2048,128]{1,0:T(8,128)(2,1)} %bitcast.17), custom_call_target="tpu_custom_call" | custom-call | flops 314572800 | bytes 5000000 | tf_op jit(solution)/shard_map/partial_sums/pallas_call | solution.py:194
  69.6 4.5 %all-to-all-start.1 = ((bf16[8,416,128]{2,1,0:T(8,128)(2,1)}), bf16[8,416,128]{2,1,0:T(8,128)(2,1)S(1)}, u32[]{:S(2)}, u32[]{:S(2)}) async-start(bf16[8,416,128]{2,1,0:T(8,128)(2,1)} %bitcast.16), calls=%async_computation.1 | async-start | bytes 1703936 | tf_op jit(solution)/shard_map/all_to_all | solution.py:388
  74.1 0.1 select_maximum_fusion.1
  74.2 0.7 select_maximum_fusion.couple_ref
  74.9 1.0 fusion.2.factor_ref
  75.9 12.0 %all-to-all-done.1.parts_ref = bf16[8,416,128]{2,1,0:T(8,128)(2,1)S(1)} async-done(((bf16[8,416,128]{2,1,0:T(8,128)(2,1)}), bf16[8,416,128]{2,1,0:T(8,128)(2,1)S(1)}, u32[]{:S(2)}, u32[]{:S(2)}) %all-to-all-start.1) | async-done | bytes 852000 | tf_op jit(solution)/shard_map/all_to_all | solution.py:388
  88.0 0.9 copy-done
  88.9 2.3 %couple_levels.1 = bf16[416,128]{1,0:T(8,128)(2,1)} custom-call(bf16[8,416,128]{2,1,0:T(8,128)(2,1)} %copy-done, f32[416,128]{1,0:T(8,128)} %fusion.2.factor_ref, f32[128,128]{1,0:T(8,128)} %select_maximum_fusion.couple_ref), custom_call_target="tpu_custom_call" | custom-call | flops 81788928 | bytes 1200000 | tf_op jit(solution)/shard_map/couple_levels/pallas_call | solution.py:230
  91.2 14.7 %all_gather.3.all_ref = bf16[3328,128]{1,0:T(8,128)(2,1)} all-gather(bf16[416,128]{1,0:T(8,128)(2,1)} %couple_levels.1), channel_id=1, replica_groups=mesh['lat'=8,'wave'=64] {'lat'}, dimensions={0}, use_global_device_ids=true | all-gather | bytes 958464 | tf_op jit(solution)/shard_map/all_gather | solution.py:390
  105.9 6.7 %inverse_sums.1 = (bf16[10,80,128]{2,1,0:T(8,128)(2,1)}, bf16[2048,128]{1,0:T(8,128)(2,1)}) custom-call(s32[10]{0:T(128)} %copy-done.2, s32[1]{0:T(128)} %dynamic_slice.7.block_ref, bf16[10,192,640]{2,1,0:T(8,128)(2,1)} %get-tuple-element.8.straight_ref, bf16[3328,128]{1,0:T(8,128)(2,1)} %all_gather.3.all_ref), custom_call_target="tpu_custom_call" | custom-call | flops 314572800 | bytes 5000000 | tf_op jit(solution)/shard_map/inverse_sums/pallas_call | solution.py:278
  112.6 39.2 %all_to_all.15 = bf16[64,32,128]{2,1,0:T(8,128)(2,1)} all-to-all(bf16[64,32,128]{2,1,0:T(8,128)(2,1)} %bitcast.21), channel_id=1, replica_groups=mesh['lat'=8,'wave'=64] {'wave'}, dimensions={0} | all-to-all | bytes 1048576 | tf_op jit(solution)/shard_map/all_to_all | solution.py:392
  151.8 7.0 %finish_rows.1 = bf16[192,2560]{1,0:T(8,128)(2,1)} custom-call(bf16[2048,128]{1,0:T(8,128)(2,1)} %bitcast.18, bf16[2,640,2560]{2,1,0:T(8,128)(2,1)} %get-tuple-element.13.table_ref), custom_call_target="tpu_custom_call" | custom-call | flops 1258291200 | bytes 9000000 | tf_op jit(solution)/shard_map/finish_rows/pallas_call | solution.py:331
  (18 shorter events, 0.3 us)
Async XLA Ops:
  2.5 50.9 %copy-start.3 = (f32[32,32]{1,0:T(8,128)S(1)}, f32[32,32]{1,0:T(8,128)}, u32[]{:S(2)}) copy-start(f32[32,32]{1,0:T(8,128)} %param.10) | copy-start | bytes 12292
  2.5 50.9 %copy-start.4 = (f32[32,32]{1,0:T(8,128)S(1)}, f32[32,32]{1,0:T(8,128)}, u32[]{:S(2)}) copy-start(f32[32,32]{1,0:T(8,128)} %param.11) | copy-start | bytes 12292
  2.5 51.0 %copy-start.5 = (s32[8]{0:T(128)S(1)}, s32[8]{0:T(128)}, u32[]{:S(2)}) copy-start(s32[8]{0:T(128)} %param.9) | copy-start | bytes 100
  12.5 50.5 %all-to-all-start = ((bf16[64,32,128]{2,1,0:T(8,128)(2,1)}), bf16[64,32,128]{2,1,0:T(8,128)(2,1)S(1)}, u32[]{:S(2)}, u32[]{:S(2)}) async-start(bf16[64,32,128]{2,1,0:T(8,128)(2,1)} %bitcast.20), calls=%async_computation | async-start | bytes 1048576 | tf_op jit(solution)/shard_map/all_to_all | solution.py:383
  32.1 13.2 %copy-start.2 = (s32[10]{0:T(128)}, s32[10]{0:T(128)S(1)}, u32[]{:S(2)}) copy-start(s32[10]{0:T(128)S(1)} %dynamic_slice.6.own_ref) | copy-start | bytes 124
  63.0 0.8 copy-start.1
  69.6 18.3 %all-to-all-start.1 = ((bf16[8,416,128]{2,1,0:T(8,128)(2,1)}), bf16[8,416,128]{2,1,0:T(8,128)(2,1)S(1)}, u32[]{:S(2)}, u32[]{:S(2)}) async-start(bf16[8,416,128]{2,1,0:T(8,128)(2,1)} %bitcast.16), calls=%async_computation.1 | async-start | bytes 1703936 | tf_op jit(solution)/shard_map/all_to_all | solution.py:388
  88.0 0.9 copy-start

commit v2 on v1

v2 whole, which is shorter than its diff:
```python
import functools
import math

import jax
import jax.numpy as jnp
from jax import lax
from jax.experimental import pallas as pl
from jax.experimental.pallas import tpu as pltpu
from jax.sharding import PartitionSpec as P

F32 = jnp.float32
BF16 = jnp.bfloat16
NLON = 2560
WAVES = 64
GROUPS = 8
SLOTS = 10
ROWS = 3
FIELDS = 64
K = 128
TOP = 640
BAND = 192
CHUNK = 32
UNIT = 16
UNITS = TOP // UNIT
PAIR_ROWS = TOP + UNIT
PACKED = 3328
SHARE = PACKED // GROUPS
VMEM_LIMIT = 24 * 1024 * 1024


def params():
    return pltpu.CompilerParams(
        dimension_semantics=("arbitrary",), vmem_limit_bytes=VMEM_LIMIT
    )


def cos_sin(phase):
    quarter = (
        (phase >= 320.0).astype(F32)
        + (phase >= 960.0).astype(F32)
        + (phase >= 1600.0).astype(F32)
        + (phase >= 2240.0).astype(F32)
    )
    x = (phase - 640.0 * quarter) * (2.0 * math.pi / NLON)
    y = x * x
    s = x * (
        1.0 + y * (-1.0 / 6 + y * (1.0 / 120 + y * (-1.0 / 5040 + y * (1.0 / 362880))))
    )
    c = 1.0 + y * (
        -0.5 + y * (1.0 / 24 + y * (-1.0 / 720 + y * (1.0 / 40320 + y * (-1.0 / 3628800))))
    )
    odd = (quarter == 1.0) | (quarter == 3.0)
    cos = jnp.where(odd, s, c)
    sin = jnp.where(odd, c, s)
    cos = jnp.where((quarter == 1.0) | (quarter == 2.0), -cos, cos)
    sin = jnp.where((quarter == 2.0) | (quarter == 3.0), -sin, sin)
    return cos, sin


def phase_of(product):
    return product - NLON * jnp.floor((product + 0.5) * (1.0 / NLON))


def forward_kernel(waves_ref, grid_ref, send_ref, table, lines, rows):
    step = pl.program_id(0)
    waves = waves_ref[...].astype(F32)
    down = lax.broadcasted_iota(jnp.int32, (128, 128), 0).astype(F32)
    near_c, near_s = cos_sin(phase_of(waves * down))
    far_c, far_s = cos_sin(phase_of(waves * (down[: NLON // 128 + 4] * 128.0)))
    factor = 1.0 / math.sqrt(NLON)
    far_c = far_c * factor
    far_s = far_s * factor
    for a in range(NLON // 128):
        ca = far_c[a : a + 1]
        sa = far_s[a : a + 1]
        at = slice(a * 128, (a + 1) * 128)
        table[at, :128] = (ca * near_c - sa * near_s).astype(BF16)
        table[at, 128:] = (-(sa * near_c) - ca * near_s).astype(BF16)
    made = jnp.dot(grid_ref[...], table[...], preferred_element_type=F32)
    at = pl.ds(pl.multiple_of(step * 128, 128), 128)
    for li in range(ROWS):
        one = made[li * FIELDS : (li + 1) * FIELDS]
        lines[li, at, :] = jnp.concatenate([one[:, :128], one[:, 128:]], axis=0).T

    @pl.when(step == 4)
    def _():
        for li in range(ROWS):
            for slot in range(SLOTS):
                rows[pl.ds(slot * ROWS + li, WAVES, stride=CHUNK), :] = lines[
                    li, pl.ds(slot, WAVES, stride=SLOTS), :
                ]
        for row in range(SLOTS * ROWS, CHUNK):
            rows[pl.ds(row, WAVES, stride=CHUNK), :] = jnp.zeros((WAVES, K), F32)
        send_ref[...] = rows[...].astype(BF16)


def forward(waves, grid):
    return pl.pallas_call(
        forward_kernel,
        grid=(5,),
        in_specs=[
            pl.BlockSpec((1, 128), lambda i: (0, i)),
            pl.BlockSpec((ROWS * FIELDS, NLON), lambda i: (0, 0)),
        ],
        out_specs=pl.BlockSpec((WAVES * CHUNK, K), lambda i: (0, 0)),
        out_shape=jax.ShapeDtypeStruct((WAVES * CHUNK, K), BF16),
        scratch_shapes=[
            pltpu.VMEM((NLON, 256), BF16),
            pltpu.VMEM((ROWS, TOP, K), F32),
            pltpu.VMEM((WAVES * CHUNK, K), F32),
        ],
        compiler_params=params(),
        cost_estimate=pl.CostEstimate(
            flops=2 * 192 * 2560 * 1280, bytes_accessed=2000000, transcendentals=0
        ),
        name="forward_rows",
    )(waves, grid)


def table_kernel(waves_ref, table_ref):
    waves = waves_ref[...]
    lanes = lax.broadcasted_iota(jnp.int32, waves.shape, 1).astype(F32)
    near_c, near_s = cos_sin(phase_of(waves * lanes))
    far_c, far_s = cos_sin(phase_of(waves * (lanes * 128.0)))
    factor = 1.0 / math.sqrt(NLON)
    far_c = far_c * factor
    far_s = far_s * factor
    for a in range(NLON // 128):
        ca = far_c[:, a : a + 1]
        sa = far_s[:, a : a + 1]
        at = slice(a * 128, (a + 1) * 128)
        table_ref[0, :, at] = (ca * near_c - sa * near_s).astype(BF16)
        table_ref[1, :, at] = (-(sa * near_c) - ca * near_s).astype(BF16)


def inverse_table(waves):
    return pl.pallas_call(
        table_kernel,
        grid=(5,),
        in_specs=[pl.BlockSpec((128, 128), lambda i: (i, 0))],
        out_specs=pl.BlockSpec((2, 128, NLON), lambda i: (0, i, 0)),
        out_shape=jax.ShapeDtypeStruct((2, TOP, NLON), BF16),
        compiler_params=params(),
        cost_estimate=pl.CostEstimate(
            flops=30000000, bytes_accessed=12000000, transcendentals=0
        ),
        name="inverse_table",
    )(waves)


def basis_kernel(own_ref, leg_ref, straight_ref, turned_ref, rows, joined):
    wave = own_ref[pl.program_id(0)]
    for b in range(TOP // 128):
        at = slice(b * 128, (b + 1) * 128)
        degree = b * 128 + lax.broadcasted_iota(jnp.int32, (BAND, 128), 1)
        rows[b] = jnp.where(degree >= wave, leg_ref[0, :, at].astype(F32), 0.0)
        for li in range(ROWS):
            joined[li * WAVES : (li + 1) * WAVES, at] = rows[
                b, pl.ds(li, WAVES, stride=ROWS), :
            ]
    straight_ref[0] = joined[...].astype(BF16)
    turned_ref[0] = joined[...].T.astype(BF16)


def basis(own, legendre):
    return pl.pallas_call(
        basis_kernel,
        grid=(SLOTS,),
        in_specs=[
            pl.BlockSpec(memory_space=pltpu.SMEM),
            pl.BlockSpec((1, BAND, TOP), lambda i: (i, 0, 0)),
        ],
        out_specs=[
            pl.BlockSpec((1, BAND, TOP), lambda i: (i, 0, 0)),
            pl.BlockSpec((1, TOP, BAND), lambda i: (i, 0, 0)),
        ],
        out_shape=[
            jax.ShapeDtypeStruct((SLOTS, BAND, TOP), BF16),
            jax.ShapeDtypeStruct((SLOTS, TOP, BAND), BF16),
        ],
        scratch_shapes=[
            pltpu.VMEM((TOP // 128, BAND, 128), F32),
            pltpu.VMEM((BAND, TOP), F32),
        ],
        compiler_params=params(),
        cost_estimate=pl.CostEstimate(
            flops=0, bytes_accessed=30000000, transcendentals=0
        ),
        name="basis_rows",
    )(own, legendre)


def partial_kernel(own_ref, turned_ref, got_ref, packed_ref, rows, held):
    step = pl.program_id(0)
    pair = 4 - step

    @pl.when(step == 0)
    def _():
        rows[...] = got_ref[...].astype(F32)
        held[TOP + 5 * PAIR_ROWS :, :] = jnp.zeros((PACKED - 5 * PAIR_ROWS, K), BF16)

    def product(q):
        slot = 2 * pair + q
        values = jnp.concatenate(
            [
                rows[pl.ds(slot * ROWS + li, WAVES, stride=CHUNK), :]
                for li in range(ROWS)
            ],
            axis=0,
        ).astype(BF16)
        return jnp.dot(turned_ref[q], values, preferred_element_type=F32).astype(BF16)

    unit = own_ref[2 * pair] // UNIT
    base = TOP + pair * PAIR_ROWS
    held[pl.ds(pl.multiple_of(base + UNIT, UNIT), TOP), :] = product(0)
    at = pl.multiple_of(base - (UNITS - 1 - unit) * UNIT, UNIT)
    held[pl.ds(at, TOP), :] = product(1)

    @pl.when(step == 4)
    def _():
        packed_ref[...] = held[TOP:, :]


def partial_sums(own, turned, got):
    return pl.pallas_call(
        partial_kernel,
        grid=(5,),
        in_specs=[
            pl.BlockSpec(memory_space=pltpu.SMEM),
            pl.BlockSpec((2, TOP, BAND), lambda i: (4 - i, 0, 0)),
            pl.BlockSpec((WAVES * CHUNK, K), lambda i: (0, 0)),
        ],
        out_specs=pl.BlockSpec((PACKED, K), lambda i: (0, 0)),
        out_shape=jax.ShapeDtypeStruct((PACKED, K), BF16),
        scratch_shapes=[
            pltpu.VMEM((WAVES * CHUNK, K), F32),
            pltpu.VMEM((TOP + PACKED, K), BF16),
        ],
        compiler_params=params(),
        cost_estimate=pl.CostEstimate(
            flops=2 * 10 * 192 * 640 * 128, bytes_accessed=5000000, transcendentals=0
        ),
        name="partial_sums",
    )(own, turned, got)


def couple_kernel(own_ref, lat_ref, parts_ref, couple_ref, out_ref):
    total = parts_ref[0].astype(F32)
    for g in range(1, GROUPS):
        total = total + parts_ref[g].astype(F32)
    pulled = jnp.dot(
        total,
        couple_ref[...],
        preferred_element_type=F32,
        precision=lax.Precision.HIGHEST,
    )
    position = lat_ref[0] * SHARE + lax.broadcasted_iota(jnp.int32, (SHARE, K), 0)
    degree = jnp.zeros((SHARE, K), jnp.int32)
    for pair in range(SLOTS // 2):
        unit = own_ref[2 * pair] // UNIT
        inside = position - pair * PAIR_ROWS
        shift = jnp.where(inside >= (unit + 1) * UNIT, -UNIT, (UNITS - 1 - unit) * UNIT)
        degree = jnp.where(inside >= 0, inside + shift, degree)
    degree = degree.astype(F32)
    column = lax.broadcasted_iota(jnp.int32, (SHARE, K), 1)
    factor = jnp.where(
        (column & 63) < 32, degree * (degree + 1.0) / float(TOP * TOP), 1.0
    )
    out_ref[...] = (total - factor * pulled).astype(BF16)


def couple(own, lat, parts, matrix):
    return pl.pallas_call(
        couple_kernel,
        in_specs=[
            pl.BlockSpec(memory_space=pltpu.SMEM),
            pl.BlockSpec(memory_space=pltpu.SMEM),
            pl.BlockSpec(memory_space=pltpu.VMEM),
            pl.BlockSpec(memory_space=pltpu.VMEM),
        ],
        out_specs=pl.BlockSpec(memory_space=pltpu.VMEM),
        out_shape=jax.ShapeDtypeStruct((SHARE, K), BF16),
        compiler_params=pltpu.CompilerParams(vmem_limit_bytes=VMEM_LIMIT),
        cost_estimate=pl.CostEstimate(
            flops=2 * 416 * 128 * 128 * 6, bytes_accessed=1200000, transcendentals=0
        ),
        name="couple_levels",
    )(own, lat, parts, matrix)


def inverse_kernel(own_ref, block_ref, straight_ref, all_ref, out_ref, send_ref, held, rows):
    step = pl.program_id(0)

    @pl.when(step == 0)
    def _():
        held[:TOP, :] = jnp.zeros((TOP, K), BF16)
        held[TOP:, :] = all_ref[...]

    base = TOP + step * PAIR_ROWS
    unit = own_ref[2 * step] // UNIT
    size = TOP // GROUPS
    begin = block_ref[0] * size
    degree = begin + lax.broadcasted_iota(jnp.int32, (size, K), 0)
    for q in range(2):
        wave = own_ref[2 * step + q]
        start = base + UNIT if q == 0 else base - (UNITS - 1 - unit) * UNIT
        values = held[pl.ds(pl.multiple_of(start, UNIT), TOP), :]
        back = jnp.dot(straight_ref[q], values, preferred_element_type=F32)
        back = back * jnp.where(wave == 0, 1.0, 2.0)
        for li in range(ROWS):
            at = (2 * step + q) * ROWS + li
            rows[pl.ds(at, WAVES, stride=CHUNK), :] = back[li * WAVES : (li + 1) * WAVES]
        mine = held[pl.ds(pl.multiple_of(start + begin, UNIT), size), :]
        out_ref[q] = jnp.where(degree >= wave, mine.astype(F32), 0.0).astype(BF16)

    @pl.when(step == 4)
    def _():
        for at in range(SLOTS * ROWS, CHUNK):
            rows[pl.ds(at, WAVES, stride=CHUNK), :] = jnp.zeros((WAVES, K), F32)
        send_ref[...] = rows[...].astype(BF16)


def inverse(own, block, straight, everything):
    return pl.pallas_call(
        inverse_kernel,
        grid=(5,),
        in_specs=[
            pl.BlockSpec(memory_space=pltpu.SMEM),
            pl.BlockSpec(memory_space=pltpu.SMEM),
            pl.BlockSpec((2, BAND, TOP), lambda i: (i, 0, 0)),
            pl.BlockSpec((PACKED, K), lambda i: (0, 0)),
        ],
        out_specs=[
            pl.BlockSpec((2, TOP // GROUPS, K), lambda i: (i, 0, 0)),
            pl.BlockSpec((WAVES * CHUNK, K), lambda i: (0, 0)),
        ],
        out_shape=[
            jax.ShapeDtypeStruct((SLOTS, TOP // GROUPS, K), BF16),
            jax.ShapeDtypeStruct((WAVES * CHUNK, K), BF16),
        ],
        scratch_shapes=[
            pltpu.VMEM((TOP + PACKED, K), BF16),
            pltpu.VMEM((WAVES * CHUNK, K), F32),
        ],
        compiler_params=params(),
        cost_estimate=pl.CostEstimate(
            flops=2 * 10 * 192 * 640 * 128, bytes_accessed=5000000, transcendentals=0
        ),
        name="inverse_sums",
    )(own, block, straight, everything)


def finish_kernel(got_ref, table_ref, out_ref, rows, left):
    @pl.when(pl.program_id(0) == 0)
    def _():
        rows[...] = got_ref[...].astype(F32)
        for li in range(ROWS):
            values = jnp.concatenate(
                [
                    rows[pl.ds(slot * ROWS + li, WAVES, stride=CHUNK), :]
                    for slot in range(SLOTS)
                ],
                axis=0,
            )
            turned = values.T.astype(BF16)
            at = slice(li * FIELDS, (li + 1) * FIELDS)
            left[at, :TOP] = turned[:FIELDS]
            left[at, TOP:] = turned[FIELDS:]

    table = table_ref[...].reshape(2 * TOP, table_ref.shape[2])
    out_ref[...] = jnp.dot(left[...], table, preferred_element_type=F32).astype(BF16)


def finish(got, table):
    block = 512
    return pl.pallas_call(
        finish_kernel,
        grid=(NLON // block,),
        in_specs=[
            pl.BlockSpec((WAVES * CHUNK, K), lambda i: (0, 0)),
            pl.BlockSpec((2, TOP, block), lambda i: (0, 0, i)),
        ],
        out_specs=pl.BlockSpec((ROWS * FIELDS, block), lambda i: (0, i)),
        out_shape=jax.ShapeDtypeStruct((ROWS * FIELDS, NLON), BF16),
        scratch_shapes=[
            pltpu.VMEM((WAVES * CHUNK, K), F32),
            pltpu.VMEM((ROWS * FIELDS, 2 * TOP), BF16),
        ],
        compiler_params=params(),
        cost_estimate=pl.CostEstimate(
            flops=2 * 192 * 2560 * 1280, bytes_accessed=9000000, transcendentals=0
        ),
        name="finish_rows",
    )(got, table)


def coupling_matrix(couple_div, couple_temp):
    zero = jnp.zeros_like(couple_div)
    one = jnp.block([[zero, couple_temp.T], [couple_div.T, zero]])
    none = jnp.zeros_like(one)
    return jnp.block([[one, none], [none, one]])


def body(grid_in, legendre, wave_order, block_order, couple_div, couple_temp):
    lat = lax.axis_index("lat")
    wave = lax.axis_index("wave")
    send = forward(wave_order.reshape(1, TOP), grid_in.reshape(ROWS * FIELDS, NLON))
    swap = functools.partial(lax.all_to_all, split_axis=0, concat_axis=0, tiled=True)
    got = swap(send.reshape(WAVES, CHUNK, K), "wave")
    own = lax.dynamic_slice_in_dim(wave_order, wave * SLOTS, SLOTS)
    block = lax.dynamic_slice_in_dim(block_order, lat, 1)
    straight, turned = basis(own, legendre)
    waves = wave_order.reshape(WAVES, SLOTS).T.reshape(TOP, 1).astype(F32)
    table = inverse_table(jnp.broadcast_to(waves, (TOP, 128)))
    matrix = coupling_matrix(couple_div, couple_temp)
    packed = partial_sums(own, turned, got.reshape(WAVES * CHUNK, K))
    parts = swap(packed.reshape(GROUPS, SHARE, K), "lat")
    spectral = couple(own, lat.reshape(1), parts, matrix)
    everything = lax.all_gather(spectral, "lat", axis=0, tiled=True)
    spectral_out, send = inverse(own, block, straight, everything)
    got = swap(send.reshape(WAVES, CHUNK, K), "wave")
    grid_out = finish(got.reshape(WAVES * CHUNK, K), table)
    return spectral_out.transpose(1, 0, 2), grid_out.reshape(ROWS, FIELDS, NLON)


def solution(mesh):
    placed = (P(("lat", "wave"), None, None), P("wave", "lat", None), P(), P(), P(), P())
    return jax.shard_map(
        body,
        mesh=mesh,
        in_specs=placed,
        out_specs=(P("lat", "wave", None), P(("lat", "wave"), None, None)),
        check_vma=False,
    )
```

time: 160 us -> 149 us (0.931)
  waiting for transfers between devices: 20.8 us -> 62.2 us
  blocking collectives: 54 us -> 13.6 us
  between operations: 13.3 us -> 0.74 us
  Pallas kernels: 39.8 us -> 29.3 us
  starting transfers between devices: 23.3 us -> 30.5 us
  local copies, waits for them, and re-layouts: 5.12 us -> 12 us
  other arithmetic: 2.5 us -> 0.16 us
    all_to_all x1 -> x2, waiting for transfers between devices: 8.79 us -> 49.3 us  [body(): got = swap(send.reshape(WAVES, CHUNK, K), 'wave')]
    all_to_all x1 -> x0, blocking collectives: 39.2 us -> none  [body(): got = swap(send.reshape(WAVES, CHUNK, K), 'wave')]
    unnamed x14 -> x22, local copies, waits for them, and re-layouts: 1.88 us -> 10.1 us
    all_to_all x1 -> x2, starting transfers between devices: 18.8 us -> 25.9 us  [body(): got = swap(send.reshape(WAVES, CHUNK, K), 'wave')]
    pallas_call x1, Pallas kernels: 8.06 us -> 2.92 us  [basis(): pl.pallas_call(basis_kernel, grid=(SLOTS,), in_specs=[pl.BlockSpec(memory...]
    pallas_call x1, Pallas kernels: 6.97 us -> 4.23 us  [finish(): pl.pallas_call(finish_kernel, grid=(NLON // block,), in_specs=[pl.BlockSp...]
    pallas_call x1, Pallas kernels: 6.68 us -> 4.78 us  [inverse(): pl.pallas_call(inverse_kernel, grid=(5,), in_specs=[pl.BlockSpec(memory_s...]
    pallas_call x2 -> x3, Pallas kernels: 12.3 us -> 13.1 us  [the longest x1 6.89 us: forward(): pl.pallas_call(forward_kernel, grid=(5,), in_specs=[pl.BlockSpec((1, 128)...]
  transfers between devices with their start and end apart: 2 -> 3, of which waited for: 2 -> 3; matrix products, arithmetic and copies ran while one was open for 3% -> 1% of each run, Pallas kernels for 5% -> 5%
where the time goes in v2:
time: 149 us; the launch traced here: 148 us
  waiting for transfers between devices  62.2 us (42%)
  starting transfers between devices  30.5 us (20%)
  Pallas kernels  29.3 us (20%)
  blocking collectives  13.6 us (9%)
  local copies, waits for them, and re-layouts  12 us (8%)
    all_to_all x2, waiting for transfers between devices, body(): got = swap(send.reshape(WAVES, CHUNK, K), 'wave')  49.3 us
    all_to_all x2, starting transfers between devices, body(): got = swap(send.reshape(WAVES, CHUNK, K), 'wave')  25.9 us
    all_gather x1, blocking collectives, body(): everything = lax.all_gather(spectral, 'lat', axis=0, tiled=True)  13.6 us
    all_to_all x1, waiting for transfers between devices, body(): parts = swap(packed.reshape(GROUPS, SHARE, K), 'lat')  12.9 us
    unnamed x22, local copies, waits for them, and re-layouts  10.1 us
    pallas_call x1, Pallas kernels, forward(): pl.pallas_call(forward_kernel, grid=(5,), in_specs=[pl.BlockSpec((1, 128)...  6.89 us
    pallas_call x1, Pallas kernels, inverse_table(): pl.pallas_call(table_kernel, grid=(5,), in_specs=[pl.BlockSpec((128, 128)...  5.15 us
    pallas_call x1, Pallas kernels, inverse(): pl.pallas_call(inverse_kernel, grid=(5,), in_specs=[pl.BlockSpec(memory_s...  4.78 us
  transfers between devices with their start and end apart: 3, of which 3 were waited for; matrix products, arithmetic and copies ran while one was open for 1% of the time, Pallas kernels for 5%

profile of v2, /device:TPU:6, one launch (start us, length us, event | category | flops | bytes accessed | tf_op | source)
XLA Modules:
  0.0 148.5 jit_solution(16227340407767234798)
XLA Ops:
  0.6 0.8 reshape.43.waves_ref
  1.4 1.2 copy-done.5
  2.6 6.9 %forward_rows.1 = bf16[2048,128]{1,0:T(8,128)(2,1)} custom-call(s32[1,640]{1,0:T(1,128)S(1)} %reshape.43.waves_ref, bf16[192,2560]{1,0:T(8,128)(2,1)S(1)} %bitcast.13), custom_call_target="tpu_custom_call" | custom-call | flops 1258291200 | bytes 2000000 | tf_op jit(solution)/shard_map/forward_rows/pallas_call | solution.py:98
  9.5 19.0 %all-to-all-start = ((bf16[64,32,128]{2,1,0:T(8,128)(2,1)}), bf16[64,32,128]{2,1,0:T(8,128)(2,1)}, u32[]{:S(2)}, u32[]{:S(2)}) async-start(bf16[64,32,128]{2,1,0:T(8,128)(2,1)} %bitcast.2), calls=%async_computation | async-start | bytes 1048576 | tf_op jit(solution)/shard_map/all_to_all | solution.py:409
  28.6 1.7 %copy-done.4 = bf16[10,192,640]{2,1,0:T(8,128)(2,1)S(1)} copy-done((bf16[10,192,640]{2,1,0:T(8,128)(2,1)S(1)}, bf16[10,192,640]{2,1,0:T(8,128)(2,1)}, u32[]{:S(2)}) %copy-start.4) | copy-done | bytes 2457624
  30.3 2.9 %basis_rows.1 = (bf16[10,192,640]{2,1,0:T(8,128)(2,1)S(1)}, bf16[10,640,192]{2,1,0:T(8,128)(2,1)S(1)}) custom-call(s32[10]{0:T(128)S(1)} %dynamic_slice.6.own_ref, bf16[10,192,640]{2,1,0:T(8,128)(2,1)S(1)} %copy-done.4), custom_call_target="tpu_custom_call" | custom-call | bytes 30000000 | tf_op jit(solution)/shard_map/basis_rows/pallas_call | solution.py:166
  33.2 1.5 copy-done.2
  34.7 25.4 %all-to-all-done = bf16[64,32,128]{2,1,0:T(8,128)(2,1)} async-done(((bf16[64,32,128]{2,1,0:T(8,128)(2,1)}), bf16[64,32,128]{2,1,0:T(8,128)(2,1)}, u32[]{:S(2)}, u32[]{:S(2)}) %all-to-all-start) | async-done | bytes 524320 | tf_op jit(solution)/shard_map/all_to_all | solution.py:409
  60.1 4.3 %partial_sums.1 = bf16[3328,128]{1,0:T(8,128)(2,1)} custom-call(s32[10]{0:T(128)S(1)} %dynamic_slice.6.own_ref, bf16[10,640,192]{2,1,0:T(8,128)(2,1)S(1)} %get-tuple-element.7.turned_ref, bf16[2048,128]{1,0:T(8,128)(2,1)} %bitcast.3.got_ref), custom_call_target="tpu_custom_call" | custom-call | flops 314572800 | bytes 5000000 | tf_op jit(solution)/shard_map/partial_sums/pallas_call | solution.py:225
  64.3 4.6 %all-to-all-start.1 = ((bf16[8,416,128]{2,1,0:T(8,128)(2,1)}), bf16[8,416,128]{2,1,0:T(8,128)(2,1)S(1)}, u32[]{:S(2)}, u32[]{:S(2)}) async-start(bf16[8,416,128]{2,1,0:T(8,128)(2,1)} %bitcast.4), calls=%async_computation.1 | async-start | bytes 1703936 | tf_op jit(solution)/shard_map/all_to_all | solution.py:417
  69.1 0.7 dynamic_slice.7.block_ref
  69.8 0.1 select_maximum_fusion.couple_ref
  69.9 12.9 %all-to-all-done.1.parts_ref = bf16[8,416,128]{2,1,0:T(8,128)(2,1)S(1)} async-done(((bf16[8,416,128]{2,1,0:T(8,128)(2,1)}), bf16[8,416,128]{2,1,0:T(8,128)(2,1)S(1)}, u32[]{:S(2)}, u32[]{:S(2)}) %all-to-all-start.1) | async-done | bytes 852000 | tf_op jit(solution)/shard_map/all_to_all | solution.py:417
  82.8 1.1 couple_levels.1
  83.9 13.6 %all_gather.3.all_ref = bf16[3328,128]{1,0:T(8,128)(2,1)S(1)} all-gather(bf16[416,128]{1,0:T(8,128)(2,1)S(1)} %couple_levels.1), channel_id=1, replica_groups=mesh['lat'=8,'wave'=64] {'lat'}, dimensions={0}, use_global_device_ids=true | all-gather | bytes 958464 | tf_op jit(solution)/shard_map/all_gather | solution.py:419
  97.5 4.8 %inverse_sums.1 = (bf16[10,80,128]{2,1,0:T(8,128)(2,1)}, bf16[2048,128]{1,0:T(8,128)(2,1)}) custom-call(s32[10]{0:T(128)S(1)} %dynamic_slice.6.own_ref, s32[1]{0:T(128)} %dynamic_slice.7.block_ref, bf16[10,192,640]{2,1,0:T(8,128)(2,1)S(1)} %copy-done.3, bf16[3328,128]{1,0:T(8,128)(2,1)S(1)} %all_gather.3.all_ref), custom_call_target="tpu_custom_call" | custom-call | flops 314572800 | bytes 5000000 | tf_op jit(solution)/shard_map/inverse_sums/pallas_call | solution.py:324
  102.2 6.9 %all-to-all-start.2 = ((bf16[64,32,128]{2,1,0:T(8,128)(2,1)}), bf16[64,32,128]{2,1,0:T(8,128)(2,1)S(1)}, u32[]{:S(2)}, u32[]{:S(2)}) async-start(bf16[64,32,128]{2,1,0:T(8,128)(2,1)} %bitcast.8), calls=%async_computation.2 | async-start | bytes 1048576 | tf_op jit(solution)/shard_map/all_to_all | solution.py:421
  109.1 0.1 convert_element_type.18
  109.4 0.2 broadcast_in_dim.2.waves_ref
  109.6 5.2 %inverse_table.1.table_ref = bf16[2,640,2560]{2,1,0:T(8,128)(2,1)S(1)} custom-call(f32[640,128]{1,0:T(8,128)S(1)} %broadcast_in_dim.2.waves_ref), custom_call_target="tpu_custom_call" | custom-call | flops 30000000 | bytes 12000000 | tf_op jit(solution)/shard_map/inverse_table/pallas_call | solution.py:137
  114.8 2.7 %copy-done = bf16[2,640,2560]{2,1,0:T(8,128)(2,1)} copy-done((bf16[2,640,2560]{2,1,0:T(8,128)(2,1)}, bf16[2,640,2560]{2,1,0:T(8,128)(2,1)S(1)}, u32[]{:S(2)}) %copy-start) | copy-done | bytes 6553624
  117.5 23.9 %all-to-all-done.2 = bf16[64,32,128]{2,1,0:T(8,128)(2,1)S(1)} async-done(((bf16[64,32,128]{2,1,0:T(8,128)(2,1)}), bf16[64,32,128]{2,1,0:T(8,128)(2,1)S(1)}, u32[]{:S(2)}, u32[]{:S(2)}) %all-to-all-start.2) | async-done | bytes 524320 | tf_op jit(solution)/shard_map/all_to_all | solution.py:421
  141.4 2.9 %copy-done.1 = bf16[2,640,2560]{2,1,0:T(8,128)(2,1)S(1)} copy-done((bf16[2,640,2560]{2,1,0:T(8,128)(2,1)S(1)}, bf16[2,640,2560]{2,1,0:T(8,128)(2,1)}, u32[]{:S(2)}) %copy-start.1) | copy-done | bytes 6553624
  144.2 4.2 %finish_rows.1 = bf16[192,2560]{1,0:T(8,128)(2,1)} custom-call(bf16[2048,128]{1,0:T(8,128)(2,1)S(1)} %bitcast.12, bf16[2,640,2560]{2,1,0:T(8,128)(2,1)S(1)} %copy-done.1), custom_call_target="tpu_custom_call" | custom-call | flops 1258291200 | bytes 9000000 | tf_op jit(solution)/shard_map/finish_rows/pallas_call | solution.py:376
  (22 shorter events, 0.5 us)
Async XLA Ops:
  0.6 27.8 %copy-start.8 = (s32[640]{0:T(1024)S(1)}, s32[640]{0:T(1024)}, u32[]{:S(2)}) copy-start(s32[640]{0:T(1024)} %param.8) | copy-start | bytes 7684
  1.4 1.2 copy-start.5
  9.5 50.6 %all-to-all-start = ((bf16[64,32,128]{2,1,0:T(8,128)(2,1)}), bf16[64,32,128]{2,1,0:T(8,128)(2,1)}, u32[]{:S(2)}, u32[]{:S(2)}) async-start(bf16[64,32,128]{2,1,0:T(8,128)(2,1)} %bitcast.2), calls=%async_computation | async-start | bytes 1048576 | tf_op jit(solution)/shard_map/all_to_all | solution.py:409
  28.6 1.7 %copy-start.4 = (bf16[10,192,640]{2,1,0:T(8,128)(2,1)S(1)}, bf16[10,192,640]{2,1,0:T(8,128)(2,1)}, u32[]{:S(2)}) copy-start(bf16[10,192,640]{2,1,0:T(8,128)(2,1)} %leg_ref.1) | copy-start | bytes 7372804
  33.2 1.5 copy-start.2
  34.7 34.3 %copy-start.6 = (f32[32,32]{1,0:T(8,128)S(1)}, f32[32,32]{1,0:T(8,128)}, u32[]{:S(2)}) copy-start(f32[32,32]{1,0:T(8,128)} %param.10) | copy-start | bytes 12292
  34.7 34.3 %copy-start.7 = (f32[32,32]{1,0:T(8,128)S(1)}, f32[32,32]{1,0:T(8,128)}, u32[]{:S(2)}) copy-start(f32[32,32]{1,0:T(8,128)} %param.11) | copy-start | bytes 12292
  34.7 34.4 %copy-start.9 = (s32[8]{0:T(128)S(1)}, s32[8]{0:T(128)}, u32[]{:S(2)}) copy-start(s32[8]{0:T(128)} %param.9) | copy-start | bytes 100
  64.3 33.1 %copy-start.3 = (bf16[10,192,640]{2,1,0:T(8,128)(2,1)S(1)}, bf16[10,192,640]{2,1,0:T(8,128)(2,1)}, u32[]{:S(2)}) copy-start(bf16[10,192,640]{2,1,0:T(8,128)(2,1)} %copy-done.2) | copy-start | bytes 7372804
  64.3 18.5 %all-to-all-start.1 = ((bf16[8,416,128]{2,1,0:T(8,128)(2,1)}), bf16[8,416,128]{2,1,0:T(8,128)(2,1)S(1)}, u32[]{:S(2)}, u32[]{:S(2)}) async-start(bf16[8,416,128]{2,1,0:T(8,128)(2,1)} %bitcast.4), calls=%async_computation.1 | async-start | bytes 1703936 | tf_op jit(solution)/shard_map/all_to_all | solution.py:417
  102.2 39.1 %all-to-all-start.2 = ((bf16[64,32,128]{2,1,0:T(8,128)(2,1)}), bf16[64,32,128]{2,1,0:T(8,128)(2,1)S(1)}, u32[]{:S(2)}, u32[]{:S(2)}) async-start(bf16[64,32,128]{2,1,0:T(8,128)(2,1)} %bitcast.8), calls=%async_computation.2 | async-start | bytes 1048576 | tf_op jit(solution)/shard_map/all_to_all | solution.py:421
  114.8 2.7 %copy-start = (bf16[2,640,2560]{2,1,0:T(8,128)(2,1)}, bf16[2,640,2560]{2,1,0:T(8,128)(2,1)S(1)}, u32[]{:S(2)}) copy-start(bf16[2,640,2560]{2,1,0:T(8,128)(2,1)S(1)} %inverse_table.1.table_ref) | copy-start | bytes 19660804
  141.4 2.9 %copy-start.1 = (bf16[2,640,2560]{2,1,0:T(8,128)(2,1)S(1)}, bf16[2,640,2560]{2,1,0:T(8,128)(2,1)}, u32[]{:S(2)}) copy-start(bf16[2,640,2560]{2,1,0:T(8,128)(2,1)} %copy-done) | copy-start | bytes 19660804

commit v3 on v2

--- a/solution.py
+++ b/solution.py
@@ -26,11 +26,13 @@
 PACKED = 3328
 SHARE = PACKED // GROUPS
 VMEM_LIMIT = 24 * 1024 * 1024
-
-
-def params():
+LARGE = 58 * 1024 * 1024
+MIDDLE = 50 * 1024 * 1024
+
+
+def params(limit=VMEM_LIMIT):
     return pltpu.CompilerParams(
-        dimension_semantics=("arbitrary",), vmem_limit_bytes=VMEM_LIMIT
+        dimension_semantics=("arbitrary",), vmem_limit_bytes=limit
     )
 
 
@@ -61,55 +63,69 @@
     return product - NLON * jnp.floor((product + 0.5) * (1.0 / NLON))
 
 
-def forward_kernel(waves_ref, grid_ref, send_ref, table, lines, rows):
-    step = pl.program_id(0)
-    waves = waves_ref[...].astype(F32)
-    down = lax.broadcasted_iota(jnp.int32, (128, 128), 0).astype(F32)
-    near_c, near_s = cos_sin(phase_of(waves * down))
-    far_c, far_s = cos_sin(phase_of(waves * (down[: NLON // 128 + 4] * 128.0)))
+def forward_kernel(waves_ref, grid_ref, send_ref, grid, table, lines, rows, sem):
+    load = pltpu.make_async_copy(grid_ref, grid, sem)
+    load.start()
     factor = 1.0 / math.sqrt(NLON)
-    far_c = far_c * factor
-    far_s = far_s * factor
-    for a in range(NLON // 128):
-        ca = far_c[a : a + 1]
-        sa = far_s[a : a + 1]
-        at = slice(a * 128, (a + 1) * 128)
-        table[at, :128] = (ca * near_c - sa * near_s).astype(BF16)
-        table[at, 128:] = (-(sa * near_c) - ca * near_s).astype(BF16)
-    made = jnp.dot(grid_ref[...], table[...], preferred_element_type=F32)
-    at = pl.ds(pl.multiple_of(step * 128, 128), 128)
+    half = NLON // 2
+    for step in range(TOP // 128):
+        waves = waves_ref[step * 128 : (step + 1) * 128].astype(F32).reshape(1, 128)
+        down = lax.broadcasted_iota(jnp.int32, (128, 128), 0).astype(F32)
+        near_c, near_s = cos_sin(phase_of(waves * down))
+        far_c, far_s = cos_sin(phase_of(waves * (down[:16] * 128.0)))
+        far_c = far_c * factor
+        far_s = far_s * factor
+        sign = 1.0 - 2.0 * (waves - 2.0 * jnp.floor(waves * 0.5))
+        held = table.at[step % 2]
+        for a in range(half // 128):
+            ca = far_c[a : a + 1]
+            sa = far_s[a : a + 1]
+            c = ca * near_c - sa * near_s
+            s = -(sa * near_c) - ca * near_s
+            at = slice(a * 128, (a + 1) * 128)
+            held[at, :128] = c.astype(BF16)
+            held[at, 128:] = s.astype(BF16)
+            at = slice(half + a * 128, half + (a + 1) * 128)
+            held[at, :128] = (c * sign).astype(BF16)
+            held[at, 128:] = (s * sign).astype(BF16)
+        if step == 0:
+            load.wait()
+        made = jnp.dot(grid[...], held[...], preferred_element_type=F32)
+        at = slice(step * 128, (step + 1) * 128)
+        for li in range(ROWS):
+            one = made[li * FIELDS : (li + 1) * FIELDS]
+            lines[li, at, :] = jnp.concatenate([one[:, :128], one[:, 128:]], axis=0).T
     for li in range(ROWS):
-        one = made[li * FIELDS : (li + 1) * FIELDS]
-        lines[li, at, :] = jnp.concatenate([one[:, :128], one[:, 128:]], axis=0).T
-
-    @pl.when(step == 4)
-    def _():
-        for li in range(ROWS):
-            for slot in range(SLOTS):
-                rows[pl.ds(slot * ROWS + li, WAVES, stride=CHUNK), :] = lines[
-                    li, pl.ds(slot, WAVES, stride=SLOTS), :
-                ]
-        for row in range(SLOTS * ROWS, CHUNK):
-            rows[pl.ds(row, WAVES, stride=CHUNK), :] = jnp.zeros((WAVES, K), F32)
-        send_ref[...] = rows[...].astype(BF16)
+        for slot in range(SLOTS):
+            rows[pl.ds(slot * ROWS + li, WAVES, stride=CHUNK), :] = lines[
+                li, pl.ds(slot, WAVES, stride=SLOTS), :
+            ]
+    clear_spare(rows)
+    send_ref[...] = rows[...].astype(BF16)
+
+
+def clear_spare(rows):
+    for row in range(SLOTS * ROWS, CHUNK):
+        rows[pl.ds(row, WAVES, stride=CHUNK), :] = jnp.zeros((WAVES, K), F32)
 
 
 def forward(waves, grid):
     return pl.pallas_call(
         forward_kernel,
-        grid=(5,),
-        in_specs=[
-            pl.BlockSpec((1, 128), lambda i: (0, i)),
-            pl.BlockSpec((ROWS * FIELDS, NLON), lambda i: (0, 0)),
-        ],
-        out_specs=pl.BlockSpec((WAVES * CHUNK, K), lambda i: (0, 0)),
+        in_specs=[
+            pl.BlockSpec(memory_space=pltpu.VMEM),
+            pl.BlockSpec(memory_space=pl.ANY),
+        ],
+        out_specs=pl.BlockSpec(memory_space=pltpu.VMEM),
         out_shape=jax.ShapeDtypeStruct((WAVES * CHUNK, K), BF16),
         scratch_shapes=[
-            pltpu.VMEM((NLON, 256), BF16),
+            pltpu.VMEM((ROWS * FIELDS, NLON), BF16),
+            pltpu.VMEM((2, NLON, 256), BF16),
             pltpu.VMEM((ROWS, TOP, K), F32),
             pltpu.VMEM((WAVES * CHUNK, K), F32),
-        ],
-        compiler_params=params(),
+            pltpu.SemaphoreType.DMA,
+        ],
+        compiler_params=pltpu.CompilerParams(vmem_limit_bytes=LARGE),
         cost_estimate=pl.CostEstimate(
             flops=2 * 192 * 2560 * 1280, bytes_accessed=2000000, transcendentals=0
         ),
@@ -140,7 +156,7 @@
         in_specs=[pl.BlockSpec((128, 128), lambda i: (i, 0))],
         out_specs=pl.BlockSpec((2, 128, NLON), lambda i: (0, i, 0)),
         out_shape=jax.ShapeDtypeStruct((2, TOP, NLON), BF16),
-        compiler_params=params(),
+        compiler_params=params(LARGE),
         cost_estimate=pl.CostEstimate(
             flops=30000000, bytes_accessed=12000000, transcendentals=0
         ),
@@ -190,17 +206,20 @@
     )(own, legendre)
 
 
-def partial_kernel(own_ref, turned_ref, got_ref, packed_ref, rows, held):
-    step = pl.program_id(0)
-    pair = 4 - step
-
-    @pl.when(step == 0)
-    def _():
-        rows[...] = got_ref[...].astype(F32)
-        held[TOP + 5 * PAIR_ROWS :, :] = jnp.zeros((PACKED - 5 * PAIR_ROWS, K), BF16)
-
-    def product(q):
-        slot = 2 * pair + q
+def partial_kernel(own_ref, turned_ref, got_ref, packed_ref, turned, rows, held, sems):
+    pairs = SLOTS // 2
+    loads = [
+        pltpu.make_async_copy(
+            turned_ref.at[pl.ds(2 * pair, 2)], turned.at[pl.ds(2 * pair, 2)], sems.at[pair]
+        )
+        for pair in range(pairs)
+    ]
+    for load in reversed(loads):
+        load.start()
+    rows[...] = got_ref[...].astype(F32)
+    held[TOP + pairs * PAIR_ROWS :, :] = jnp.zeros((PACKED - pairs * PAIR_ROWS, K), BF16)
+
+    def product(slot):
         values = jnp.concatenate(
             [
                 rows[pl.ds(slot * ROWS + li, WAVES, stride=CHUNK), :]
@@ -208,35 +227,35 @@
             ],
             axis=0,
         ).astype(BF16)
-        return jnp.dot(turned_ref[q], values, preferred_element_type=F32).astype(BF16)
-
-    unit = own_ref[2 * pair] // UNIT
-    base = TOP + pair * PAIR_ROWS
-    held[pl.ds(pl.multiple_of(base + UNIT, UNIT), TOP), :] = product(0)
-    at = pl.multiple_of(base - (UNITS - 1 - unit) * UNIT, UNIT)
-    held[pl.ds(at, TOP), :] = product(1)
-
-    @pl.when(step == 4)
-    def _():
-        packed_ref[...] = held[TOP:, :]
+        return jnp.dot(turned[slot], values, preferred_element_type=F32).astype(BF16)
+
+    for pair in reversed(range(pairs)):
+        unit = own_ref[2 * pair] // UNIT
+        base = TOP + pair * PAIR_ROWS
+        loads[pair].wait()
+        held[base + UNIT : base + UNIT + TOP, :] = product(2 * pair)
+        at = pl.multiple_of(base - (UNITS - 1 - unit) * UNIT, UNIT)
+        held[pl.ds(at, TOP), :] = product(2 * pair + 1)
+    packed_ref[...] = held[TOP:, :]
 
 
 def partial_sums(own, turned, got):
     return pl.pallas_call(
         partial_kernel,
-        grid=(5,),
-        in_specs=[
-            pl.BlockSpec(memory_space=pltpu.SMEM),
-            pl.BlockSpec((2, TOP, BAND), lambda i: (4 - i, 0, 0)),
-            pl.BlockSpec((WAVES * CHUNK, K), lambda i: (0, 0)),
-        ],
-        out_specs=pl.BlockSpec((PACKED, K), lambda i: (0, 0)),
+        in_specs=[
+            pl.BlockSpec(memory_space=pltpu.SMEM),
+            pl.BlockSpec(memory_space=pl.ANY),
+            pl.BlockSpec(memory_space=pltpu.VMEM),
+        ],
+        out_specs=pl.BlockSpec(memory_space=pltpu.VMEM),
         out_shape=jax.ShapeDtypeStruct((PACKED, K), BF16),
         scratch_shapes=[
+            pltpu.VMEM((SLOTS, TOP, BAND), BF16),
             pltpu.VMEM((WAVES * CHUNK, K), F32),
             pltpu.VMEM((TOP + PACKED, K), BF16),
-        ],
-        compiler_params=params(),
+            pltpu.SemaphoreType.DMA((SLOTS // 2,)),
+        ],
+        compiler_params=pltpu.CompilerParams(vmem_limit_bytes=VMEM_LIMIT),
         cost_estimate=pl.CostEstimate(
             flops=2 * 10 * 192 * 640 * 128, bytes_accessed=5000000, transcendentals=0
         ),
@@ -288,61 +307,69 @@
     )(own, lat, parts, matrix)
 
 
-def inverse_kernel(own_ref, block_ref, straight_ref, all_ref, out_ref, send_ref, held, rows):
-    step = pl.program_id(0)
-
-    @pl.when(step == 0)
-    def _():
-        held[:TOP, :] = jnp.zeros((TOP, K), BF16)
-        held[TOP:, :] = all_ref[...]
-
-    base = TOP + step * PAIR_ROWS
-    unit = own_ref[2 * step] // UNIT
+def inverse_kernel(
+    own_ref, block_ref, straight_ref, all_ref, out_ref, send_ref, straight, held, rows, sems
+):
+    pairs = SLOTS // 2
+    loads = [
+        pltpu.make_async_copy(
+            straight_ref.at[pl.ds(2 * pair, 2)], straight.at[pl.ds(2 * pair, 2)], sems.at[pair]
+        )
+        for pair in range(pairs)
+    ]
+    for load in loads:
+        load.start()
+    held[:TOP, :] = jnp.zeros((TOP, K), BF16)
+    held[TOP:, :] = all_ref[...]
     size = TOP // GROUPS
     begin = block_ref[0] * size
     degree = begin + lax.broadcasted_iota(jnp.int32, (size, K), 0)
-    for q in range(2):
-        wave = own_ref[2 * step + q]
-        start = base + UNIT if q == 0 else base - (UNITS - 1 - unit) * UNIT
-        values = held[pl.ds(pl.multiple_of(start, UNIT), TOP), :]
-        back = jnp.dot(straight_ref[q], values, preferred_element_type=F32)
-        back = back * jnp.where(wave == 0, 1.0, 2.0)
-        for li in range(ROWS):
-            at = (2 * step + q) * ROWS + li
-            rows[pl.ds(at, WAVES, stride=CHUNK), :] = back[li * WAVES : (li + 1) * WAVES]
-        mine = held[pl.ds(pl.multiple_of(start + begin, UNIT), size), :]
-        out_ref[q] = jnp.where(degree >= wave, mine.astype(F32), 0.0).astype(BF16)
-
-    @pl.when(step == 4)
-    def _():
-        for at in range(SLOTS * ROWS, CHUNK):
-            rows[pl.ds(at, WAVES, stride=CHUNK), :] = jnp.zeros((WAVES, K), F32)
-        send_ref[...] = rows[...].astype(BF16)
+    for pair in range(pairs):
+        base = TOP + pair * PAIR_ROWS
+        unit = own_ref[2 * pair] // UNIT
+        loads[pair].wait()
+        for q in range(2):
+            slot = 2 * pair + q
+            wave = own_ref[slot]
+            start = base + UNIT if q == 0 else base - (UNITS - 1 - unit) * UNIT
+            values = held[pl.ds(pl.multiple_of(start, UNIT), TOP), :]
+            back = jnp.dot(straight[slot], values, preferred_element_type=F32)
+            back = back * jnp.where(wave == 0, 1.0, 2.0)
+            for li in range(ROWS):
+                at = slot * ROWS + li
+                rows[pl.ds(at, WAVES, stride=CHUNK), :] = back[
+                    li * WAVES : (li + 1) * WAVES
+                ]
+            mine = held[pl.ds(pl.multiple_of(start + begin, UNIT), size), :]
+            out_ref[slot] = jnp.where(degree >= wave, mine.astype(F32), 0.0).astype(BF16)
+    clear_spare(rows)
+    send_ref[...] = rows[...].astype(BF16)
 
 
 def inverse(own, block, straight, everything):
     return pl.pallas_call(
         inverse_kernel,
-        grid=(5,),
-        in_specs=[
-            pl.BlockSpec(memory_space=pltpu.SMEM),
-            pl.BlockSpec(memory_space=pltpu.SMEM),
-            pl.BlockSpec((2, BAND, TOP), lambda i: (i, 0, 0)),
-            pl.BlockSpec((PACKED, K), lambda i: (0, 0)),
+        in_specs=[
+            pl.BlockSpec(memory_space=pltpu.SMEM),
+            pl.BlockSpec(memory_space=pltpu.SMEM),
+            pl.BlockSpec(memory_space=pl.ANY),
+            pl.BlockSpec(memory_space=pltpu.VMEM),
         ],
         out_specs=[
-            pl.BlockSpec((2, TOP // GROUPS, K), lambda i: (i, 0, 0)),
-            pl.BlockSpec((WAVES * CHUNK, K), lambda i: (0, 0)),
+            pl.BlockSpec(memory_space=pltpu.VMEM),
+            pl.BlockSpec(memory_space=pltpu.VMEM),
         ],
         out_shape=[
             jax.ShapeDtypeStruct((SLOTS, TOP // GROUPS, K), BF16),
             jax.ShapeDtypeStruct((WAVES * CHUNK, K), BF16),
         ],
         scratch_shapes=[
+            pltpu.VMEM((SLOTS, BAND, TOP), BF16),
             pltpu.VMEM((TOP + PACKED, K), BF16),
             pltpu.VMEM((WAVES * CHUNK, K), F32),
-        ],
-        compiler_params=params(),
+            pltpu.SemaphoreType.DMA((SLOTS // 2,)),
+        ],
+        compiler_params=pltpu.CompilerParams(vmem_limit_bytes=VMEM_LIMIT),
         cost_estimate=pl.CostEstimate(
             flops=2 * 10 * 192 * 640 * 128, bytes_accessed=5000000, transcendentals=0
         ),
@@ -350,43 +377,63 @@
     )(own, block, straight, everything)
 
 
-def finish_kernel(got_ref, table_ref, out_ref, rows, left):
-    @pl.when(pl.program_id(0) == 0)
-    def _():
-        rows[...] = got_ref[...].astype(F32)
-        for li in range(ROWS):
-            values = jnp.concatenate(
-                [
-                    rows[pl.ds(slot * ROWS + li, WAVES, stride=CHUNK), :]
-                    for slot in range(SLOTS)
-                ],
-                axis=0,
-            )
-            turned = values.T.astype(BF16)
-            at = slice(li * FIELDS, (li + 1) * FIELDS)
-            left[at, :TOP] = turned[:FIELDS]
-            left[at, TOP:] = turned[FIELDS:]
-
-    table = table_ref[...].reshape(2 * TOP, table_ref.shape[2])
-    out_ref[...] = jnp.dot(left[...], table, preferred_element_type=F32).astype(BF16)
+def finish_kernel(got_ref, table_ref, out_ref, table, made, rows, left, loads, stores):
+    parts, _, _, block = table.shape
+
+    def load(part):
+        at = pl.ds(part * block, block)
+        return pltpu.make_async_copy(
+            table_ref.at[:, :, at], table.at[part], loads.at[part]
+        )
+
+    def store(part):
+        at = pl.ds(part * block, block)
+        return pltpu.make_async_copy(made.at[part], out_ref.at[:, at], stores.at[part])
+
+    for part in range(parts):
+        load(part).start()
+    rows[...] = got_ref[...].astype(F32)
+    for li in range(ROWS):
+        values = jnp.concatenate(
+            [
+                rows[pl.ds(slot * ROWS + li, WAVES, stride=CHUNK), :]
+                for slot in range(SLOTS)
+            ],
+            axis=0,
+        )
+        turned = values.T.astype(BF16)
+        at = slice(li * FIELDS, (li + 1) * FIELDS)
+        left[at, :TOP] = turned[:FIELDS]
+        left[at, TOP:] = turned[FIELDS:]
+    for part in range(parts):
+        load(part).wait()
+        right = table[part].reshape(2 * TOP, block)
+        made[part] = jnp.dot(left[...], right, preferred_element_type=F32).astype(BF16)
+        store(part).start()
+    for part in range(parts):
+        store(part).wait()
 
 
 def finish(got, table):
-    block = 512
+    parts = 5
+    block = NLON // parts
     return pl.pallas_call(
         finish_kernel,
-        grid=(NLON // block,),
-        in_specs=[
-            pl.BlockSpec((WAVES * CHUNK, K), lambda i: (0, 0)),
-            pl.BlockSpec((2, TOP, block), lambda i: (0, 0, i)),
-        ],
-        out_specs=pl.BlockSpec((ROWS * FIELDS, block), lambda i: (0, i)),
+        in_specs=[
+            pl.BlockSpec(memory_space=pltpu.VMEM),
+            pl.BlockSpec(memory_space=pl.ANY),
+        ],
+        out_specs=pl.BlockSpec(memory_space=pl.ANY),
         out_shape=jax.ShapeDtypeStruct((ROWS * FIELDS, NLON), BF16),
         scratch_shapes=[
+            pltpu.VMEM((parts, 2, TOP, block), BF16),
+            pltpu.VMEM((parts, ROWS * FIELDS, block), BF16),
             pltpu.VMEM((WAVES * CHUNK, K), F32),
             pltpu.VMEM((ROWS * FIELDS, 2 * TOP), BF16),
-        ],
-        compiler_params=params(),
+            pltpu.SemaphoreType.DMA((parts,)),
+            pltpu.SemaphoreType.DMA((parts,)),
+        ],
+        compiler_params=pltpu.CompilerParams(vmem_limit_bytes=MIDDLE),
         cost_estimate=pl.CostEstimate(
             flops=2 * 192 * 2560 * 1280, bytes_accessed=9000000, transcendentals=0
         ),
@@ -404,7 +451,7 @@
 def body(grid_in, legendre, wave_order, block_order, couple_div, couple_temp):
     lat = lax.axis_index("lat")
     wave = lax.axis_index("wave")
-    send = forward(wave_order.reshape(1, TOP), grid_in.reshape(ROWS * FIELDS, NLON))
+    send = forward(wave_order, grid_in.reshape(ROWS * FIELDS, NLON))
     swap = functools.partial(lax.all_to_all, split_axis=0, concat_axis=0, tiled=True)
     got = swap(send.reshape(WAVES, CHUNK, K), "wave")
     own = lax.dynamic_slice_in_dim(wave_order, wave * SLOTS, SLOTS)

time: 149 us -> 147 us (0.987)
  local copies, waits for them, and re-layouts: 12 us -> 5.23 us
  Pallas kernels: 29.3 us -> 33.5 us
    unnamed x22 -> x16, local copies, waits for them, and re-layouts: 10.1 us -> 3.3 us
    pallas_call x4, Pallas kernels: 20.2 us -> 22.6 us  [the longest x1 6.64 us: forward(): pl.pallas_call(forward_kernel, in_specs=[pl.BlockSpec(memory_space=pltpu....]
    pallas_call x1, Pallas kernels: 5.15 us -> 6.91 us  [inverse_table(): pl.pallas_call(table_kernel, grid=(5,), in_specs=[pl.BlockSpec((128, 128)...]
  transfers between devices with their start and end apart: 3 -> 3, of which waited for: 3 -> 3; matrix products, arithmetic and copies ran while one was open for 1% -> 2% of each run, Pallas kernels for 5% -> 7%
where the time goes in v3:
time: 147 us; the launch traced here: 146 us
  waiting for transfers between devices  62.4 us (42%)
  Pallas kernels  33.5 us (23%)
  starting transfers between devices  30.5 us (21%)
  blocking collectives  13.6 us (9%)
  local copies, waits for them, and re-layouts  5.23 us (4%)
    all_to_all x2, waiting for transfers between devices, body(): got = swap(send.reshape(WAVES, CHUNK, K), 'wave')  49.5 us
    all_to_all x2, starting transfers between devices, body(): got = swap(send.reshape(WAVES, CHUNK, K), 'wave')  25.9 us
    all_gather x1, blocking collectives, body(): everything = lax.all_gather(spectral, 'lat', axis=0, tiled=True)  13.6 us
    all_to_all x1, waiting for transfers between devices, body(): parts = swap(packed.reshape(GROUPS, SHARE, K), 'lat')  12.9 us
    pallas_call x1, Pallas kernels, inverse_table(): pl.pallas_call(table_kernel, grid=(5,), in_specs=[pl.BlockSpec((128, 128)...  6.91 us
    pallas_call x1, Pallas kernels, forward(): pl.pallas_call(forward_kernel, in_specs=[pl.BlockSpec(memory_space=pltpu....  6.64 us
    pallas_call x1, Pallas kernels, inverse(): pl.pallas_call(inverse_kernel, in_specs=[pl.BlockSpec(memory_space=pltpu....  5.96 us
    pallas_call x1, Pallas kernels, partial_sums(): pl.pallas_call(partial_kernel, in_specs=[pl.BlockSpec(memory_space=pltpu....  5.22 us
  transfers between devices with their start and end apart: 3, of which 3 were waited for; matrix products, arithmetic and copies ran while one was open for 2% of the time, Pallas kernels for 7%

profile of v3, /device:TPU:6, one launch (start us, length us, event | category | flops | bytes accessed | tf_op | source)
XLA Modules:
  0.0 146.3 jit_solution(18380869081816730556)
XLA Ops:
  0.6 6.6 %forward_rows.1 = bf16[2048,128]{1,0:T(8,128)(2,1)} custom-call(s32[640]{0:T(1024)} %waves_ref.1, bf16[192,2560]{1,0:T(8,128)(2,1)} %bitcast.18), custom_call_target="tpu_custom_call" | custom-call | flops 1258291200 | bytes 2000000 | tf_op jit(solution)/shard_map/forward_rows/pallas_call | solution.py:113
  7.3 19.0 %all-to-all-start = ((bf16[64,32,128]{2,1,0:T(8,128)(2,1)}), bf16[64,32,128]{2,1,0:T(8,128)(2,1)}, u32[]{:S(2)}, u32[]{:S(2)}) async-start(bf16[64,32,128]{2,1,0:T(8,128)(2,1)} %bitcast.14), calls=%async_computation | async-start | bytes 1048576 | tf_op jit(solution)/shard_map/all_to_all | solution.py:456
  26.3 0.1 dynamic_slice.6.own_ref
  26.4 1.7 %copy-done.2 = bf16[10,192,640]{2,1,0:T(8,128)(2,1)S(1)} copy-done((bf16[10,192,640]{2,1,0:T(8,128)(2,1)S(1)}, bf16[10,192,640]{2,1,0:T(8,128)(2,1)}, u32[]{:S(2)}) %copy-start.2) | copy-done | bytes 2457624
  28.1 2.9 %basis_rows.1 = (bf16[10,192,640]{2,1,0:T(8,128)(2,1)S(1)}, bf16[10,640,192]{2,1,0:T(8,128)(2,1)S(1)}) custom-call(s32[10]{0:T(128)S(1)} %dynamic_slice.6.own_ref, bf16[10,192,640]{2,1,0:T(8,128)(2,1)S(1)} %copy-done.2), custom_call_target="tpu_custom_call" | custom-call | bytes 30000000 | tf_op jit(solution)/shard_map/basis_rows/pallas_call | solution.py:182
  31.0 1.4 copy-done
  32.5 25.4 %all-to-all-done = bf16[64,32,128]{2,1,0:T(8,128)(2,1)} async-done(((bf16[64,32,128]{2,1,0:T(8,128)(2,1)}), bf16[64,32,128]{2,1,0:T(8,128)(2,1)}, u32[]{:S(2)}, u32[]{:S(2)}) %all-to-all-start) | async-done | bytes 524320 | tf_op jit(solution)/shard_map/all_to_all | solution.py:456
  57.9 5.2 %partial_sums.1 = bf16[3328,128]{1,0:T(8,128)(2,1)} custom-call(s32[10]{0:T(128)S(1)} %dynamic_slice.6.own_ref, bf16[10,640,192]{2,1,0:T(8,128)(2,1)S(1)} %get-tuple-element.7.turned_ref, bf16[2048,128]{1,0:T(8,128)(2,1)} %bitcast.3.got_ref), custom_call_target="tpu_custom_call" | custom-call | flops 314572800 | bytes 5000000 | tf_op jit(solution)/shard_map/partial_sums/pallas_call | solution.py:243
  63.1 4.6 %all-to-all-start.1 = ((bf16[8,416,128]{2,1,0:T(8,128)(2,1)}), bf16[8,416,128]{2,1,0:T(8,128)(2,1)S(1)}, u32[]{:S(2)}, u32[]{:S(2)}) async-start(bf16[8,416,128]{2,1,0:T(8,128)(2,1)} %bitcast.4), calls=%async_computation.1 | async-start | bytes 1703936 | tf_op jit(solution)/shard_map/all_to_all | solution.py:464
  67.9 0.7 dynamic_slice.7.block_ref
  68.6 0.1 select_maximum_fusion.1
  68.6 0.1 select_maximum_fusion.couple_ref
  68.7 12.9 %all-to-all-done.1.parts_ref = bf16[8,416,128]{2,1,0:T(8,128)(2,1)S(1)} async-done(((bf16[8,416,128]{2,1,0:T(8,128)(2,1)}), bf16[8,416,128]{2,1,0:T(8,128)(2,1)S(1)}, u32[]{:S(2)}, u32[]{:S(2)}) %all-to-all-start.1) | async-done | bytes 852000 | tf_op jit(solution)/shard_map/all_to_all | solution.py:464
  81.6 1.1 couple_levels.1
  82.7 13.6 %all_gather.3.all_ref = bf16[3328,128]{1,0:T(8,128)(2,1)S(1)} all-gather(bf16[416,128]{1,0:T(8,128)(2,1)S(1)} %couple_levels.1), channel_id=1, replica_groups=mesh['lat'=8,'wave'=64] {'lat'}, dimensions={0}, use_global_device_ids=true | all-gather | bytes 958464 | tf_op jit(solution)/shard_map/all_gather | solution.py:466
  96.3 6.0 %inverse_sums.1 = (bf16[10,80,128]{2,1,0:T(8,128)(2,1)}, bf16[2048,128]{1,0:T(8,128)(2,1)}) custom-call(s32[10]{0:T(128)S(1)} %dynamic_slice.6.own_ref, s32[1]{0:T(128)} %dynamic_slice.7.block_ref, bf16[10,192,640]{2,1,0:T(8,128)(2,1)S(1)} %copy-done.1, bf16[3328,128]{1,0:T(8,128)(2,1)S(1)} %all_gather.3.all_ref), custom_call_target="tpu_custom_call" | custom-call | flops 314572800 | bytes 5000000 | tf_op jit(solution)/shard_map/inverse_sums/pallas_call | solution.py:350
  102.2 6.9 %all-to-all-start.2 = ((bf16[64,32,128]{2,1,0:T(8,128)(2,1)}), bf16[64,32,128]{2,1,0:T(8,128)(2,1)S(1)}, u32[]{:S(2)}, u32[]{:S(2)}) async-start(bf16[64,32,128]{2,1,0:T(8,128)(2,1)} %bitcast.8), calls=%async_computation.2 | async-start | bytes 1048576 | tf_op jit(solution)/shard_map/all_to_all | solution.py:468
  109.2 0.1 convert_element_type.18
  109.3 0.1 copy.12
  109.4 0.1 convert_element_type.20
  109.4 0.9 broadcast_in_dim.2.waves_ref
  110.4 6.9 %inverse_table.1.table_ref = bf16[2,640,2560]{2,1,0:T(8,128)(2,1)} custom-call(f32[640,128]{1,0:T(8,128)} %broadcast_in_dim.2.waves_ref), custom_call_target="tpu_custom_call" | custom-call | flops 30000000 | bytes 12000000 | tf_op jit(solution)/shard_map/inverse_table/pallas_call | solution.py:153
  117.3 24.1 %all-to-all-done.2 = bf16[64,32,128]{2,1,0:T(8,128)(2,1)S(1)} async-done(((bf16[64,32,128]{2,1,0:T(8,128)(2,1)}), bf16[64,32,128]{2,1,0:T(8,128)(2,1)S(1)}, u32[]{:S(2)}, u32[]{:S(2)}) %all-to-all-start.2) | async-done | bytes 524320 | tf_op jit(solution)/shard_map/all_to_all | solution.py:468
  141.4 4.8 %finish_rows.1 = bf16[192,2560]{1,0:T(8,128)(2,1)} custom-call(bf16[2048,128]{1,0:T(8,128)(2,1)S(1)} %bitcast.12, bf16[2,640,2560]{2,1,0:T(8,128)(2,1)} %inverse_table.1.table_ref), custom_call_target="tpu_custom_call" | custom-call | flops 1258291200 | bytes 9000000 | tf_op jit(solution)/shard_map/finish_rows/pallas_call | solution.py:420
  (15 shorter events, 0.2 us)
Async XLA Ops:
  0.6 25.7 %copy-start.5 = (s32[640]{0:T(1024)S(1)}, s32[640]{0:T(1024)}, u32[]{:S(2)}) copy-start(s32[640]{0:T(1024)} %waves_ref.1) | copy-start | bytes 7684
  7.3 50.6 %all-to-all-start = ((bf16[64,32,128]{2,1,0:T(8,128)(2,1)}), bf16[64,32,128]{2,1,0:T(8,128)(2,1)}, u32[]{:S(2)}, u32[]{:S(2)}) async-start(bf16[64,32,128]{2,1,0:T(8,128)(2,1)} %bitcast.14), calls=%async_computation | async-start | bytes 1048576 | tf_op jit(solution)/shard_map/all_to_all | solution.py:456
  26.4 1.7 %copy-start.2 = (bf16[10,192,640]{2,1,0:T(8,128)(2,1)S(1)}, bf16[10,192,640]{2,1,0:T(8,128)(2,1)}, u32[]{:S(2)}) copy-start(bf16[10,192,640]{2,1,0:T(8,128)(2,1)} %leg_ref.1) | copy-start | bytes 7372804
  31.0 1.4 copy-start
  32.5 35.3 %copy-start.3 = (f32[32,32]{1,0:T(8,128)S(1)}, f32[32,32]{1,0:T(8,128)}, u32[]{:S(2)}) copy-start(f32[32,32]{1,0:T(8,128)} %param.10) | copy-start | bytes 12292
  32.5 35.3 %copy-start.4 = (f32[32,32]{1,0:T(8,128)S(1)}, f32[32,32]{1,0:T(8,128)}, u32[]{:S(2)}) copy-start(f32[32,32]{1,0:T(8,128)} %param.11) | copy-start | bytes 12292
  32.5 35.4 %copy-start.6 = (s32[8]{0:T(128)S(1)}, s32[8]{0:T(128)}, u32[]{:S(2)}) copy-start(s32[8]{0:T(128)} %param.9) | copy-start | bytes 100
  63.1 33.1 %copy-start.1 = (bf16[10,192,640]{2,1,0:T(8,128)(2,1)S(1)}, bf16[10,192,640]{2,1,0:T(8,128)(2,1)}, u32[]{:S(2)}) copy-start(bf16[10,192,640]{2,1,0:T(8,128)(2,1)} %copy-done) | copy-start | bytes 7372804
  63.1 18.5 %all-to-all-start.1 = ((bf16[8,416,128]{2,1,0:T(8,128)(2,1)}), bf16[8,416,128]{2,1,0:T(8,128)(2,1)S(1)}, u32[]{:S(2)}, u32[]{:S(2)}) async-start(bf16[8,416,128]{2,1,0:T(8,128)(2,1)} %bitcast.4), calls=%async_computation.1 | async-start | bytes 1703936 | tf_op jit(solution)/shard_map/all_to_all | solution.py:464
  102.2 39.2 %all-to-all-start.2 = ((bf16[64,32,128]{2,1,0:T(8,128)(2,1)}), bf16[64,32,128]{2,1,0:T(8,128)(2,1)S(1)}, u32[]{:S(2)}, u32[]{:S(2)}) async-start(bf16[64,32,128]{2,1,0:T(8,128)(2,1)} %bitcast.8), calls=%async_computation.2 | async-start | bytes 1048576 | tf_op jit(solution)/shard_map/all_to_all | solution.py:468

commit v4 on v2

--- a/solution.py
+++ b/solution.py
@@ -20,17 +20,20 @@
 TOP = 640
 BAND = 192
 CHUNK = 32
+LINE = CHUNK + 1
 UNIT = 16
 UNITS = TOP // UNIT
 PAIR_ROWS = TOP + UNIT
 PACKED = 3328
 SHARE = PACKED // GROUPS
 VMEM_LIMIT = 24 * 1024 * 1024
-
-
-def params():
+LARGE = 58 * 1024 * 1024
+MIDDLE = 50 * 1024 * 1024
+
+
+def params(limit=VMEM_LIMIT):
     return pltpu.CompilerParams(
-        dimension_semantics=("arbitrary",), vmem_limit_bytes=VMEM_LIMIT
+        dimension_semantics=("arbitrary",), vmem_limit_bytes=limit
     )
 
 
@@ -61,55 +64,100 @@
     return product - NLON * jnp.floor((product + 0.5) * (1.0 / NLON))
 
 
-def forward_kernel(waves_ref, grid_ref, send_ref, table, lines, rows):
+def forward_kernel(waves_ref, grid_ref, send_ref, grid, lines, rows, sem):
     step = pl.program_id(0)
-    waves = waves_ref[...].astype(F32)
+    load = pltpu.make_async_copy(grid_ref, grid, sem)
+
+    @pl.when(step == 0)
+    def _():
+        load.start()
+
+    waves = jnp.zeros((1, 128), F32)
+    for part in range(TOP // 128):
+        one = waves_ref[part * 128 : (part + 1) * 128].astype(F32).reshape(1, 128)
+        waves = jnp.where(step == part, one, waves)
     down = lax.broadcasted_iota(jnp.int32, (128, 128), 0).astype(F32)
     near_c, near_s = cos_sin(phase_of(waves * down))
-    far_c, far_s = cos_sin(phase_of(waves * (down[: NLON // 128 + 4] * 128.0)))
+    far_c, far_s = cos_sin(phase_of(waves * (down[:16] * 128.0)))
     factor = 1.0 / math.sqrt(NLON)
     far_c = far_c * factor
     far_s = far_s * factor
-    for a in range(NLON // 128):
+    sign = 1.0 - 2.0 * (waves - 2.0 * jnp.floor(waves * 0.5))
+
+    @pl.when(step == 0)
+    def _():
+        load.wait()
+
+    made = jnp.zeros((ROWS * FIELDS, 256), F32)
+    half = NLON // 2
+    for a in range(half // 128):
         ca = far_c[a : a + 1]
         sa = far_s[a : a + 1]
-        at = slice(a * 128, (a + 1) * 128)
-        table[at, :128] = (ca * near_c - sa * near_s).astype(BF16)
-        table[at, 128:] = (-(sa * near_c) - ca * near_s).astype(BF16)
-    made = jnp.dot(grid_ref[...], table[...], preferred_element_type=F32)
+        c = ca * near_c - sa * near_s
+        s = -(sa * near_c) - ca * near_s
+        first = jnp.concatenate([c, s], axis=1).astype(BF16)
+        second = jnp.concatenate([c * sign, s * sign], axis=1).astype(BF16)
+        left = jnp.concatenate(
+            [
+                grid[:, a * 128 : (a + 1) * 128],
+                grid[:, half + a * 128 : half + (a + 1) * 128],
+            ],
+            axis=1,
+        )
+        right = jnp.concatenate([first, second], axis=0)
+        made = made + jnp.dot(left, right, preferred_element_type=F32)
     at = pl.ds(pl.multiple_of(step * 128, 128), 128)
     for li in range(ROWS):
         one = made[li * FIELDS : (li + 1) * FIELDS]
         lines[li, at, :] = jnp.concatenate([one[:, :128], one[:, 128:]], axis=0).T
 
-    @pl.when(step == 4)
+    @pl.when(step == TOP // 128 - 1)
     def _():
         for li in range(ROWS):
             for slot in range(SLOTS):
-                rows[pl.ds(slot * ROWS + li, WAVES, stride=CHUNK), :] = lines[
+                rows[pl.ds(slot * ROWS + li, WAVES, stride=LINE), :] = lines[
                     li, pl.ds(slot, WAVES, stride=SLOTS), :
                 ]
-        for row in range(SLOTS * ROWS, CHUNK):
-            rows[pl.ds(row, WAVES, stride=CHUNK), :] = jnp.zeros((WAVES, K), F32)
-        send_ref[...] = rows[...].astype(BF16)
+        clear_spare(rows)
+        tighten(rows, send_ref)
+
+
+def clear_spare(rows):
+    for row in range(SLOTS * ROWS, CHUNK):
+        rows[pl.ds(row, WAVES, stride=LINE), :] = jnp.zeros((WAVES, K), F32)
+
+
+def tighten(rows, out):
+    for wave in range(WAVES):
+        out[wave * CHUNK : (wave + 1) * CHUNK, :] = rows[
+            wave * LINE : wave * LINE + CHUNK, :
+        ].astype(BF16)
+
+
+def loosen(got, rows):
+    for wave in range(WAVES):
+        rows[wave * LINE : wave * LINE + CHUNK, :] = got[
+            wave * CHUNK : (wave + 1) * CHUNK, :
+        ].astype(F32)
 
 
 def forward(waves, grid):
     return pl.pallas_call(
         forward_kernel,
-        grid=(5,),
+        grid=(TOP // 128,),
         in_specs=[
-            pl.BlockSpec((1, 128), lambda i: (0, i)),
-            pl.BlockSpec((ROWS * FIELDS, NLON), lambda i: (0, 0)),
+            pl.BlockSpec((TOP,), lambda i: (0,)),
+            pl.BlockSpec(memory_space=pl.ANY),
         ],
         out_specs=pl.BlockSpec((WAVES * CHUNK, K), lambda i: (0, 0)),
         out_shape=jax.ShapeDtypeStruct((WAVES * CHUNK, K), BF16),
         scratch_shapes=[
-            pltpu.VMEM((NLON, 256), BF16),
+            pltpu.VMEM((ROWS * FIELDS, NLON), BF16),
             pltpu.VMEM((ROWS, TOP, K), F32),
-            pltpu.VMEM((WAVES * CHUNK, K), F32),
-        ],
-        compiler_params=params(),
+            pltpu.VMEM((WAVES * LINE, K), F32),
+            pltpu.SemaphoreType.DMA,
+        ],
+        compiler_params=params(LARGE),
         cost_estimate=pl.CostEstimate(
             flops=2 * 192 * 2560 * 1280, bytes_accessed=2000000, transcendentals=0
         ),
@@ -140,7 +188,7 @@
         in_specs=[pl.BlockSpec((128, 128), lambda i: (i, 0))],
         out_specs=pl.BlockSpec((2, 128, NLON), lambda i: (0, i, 0)),
         out_shape=jax.ShapeDtypeStruct((2, TOP, NLON), BF16),
-        compiler_params=params(),
+        compiler_params=params(LARGE),
         cost_estimate=pl.CostEstimate(
             flops=30000000, bytes_accessed=12000000, transcendentals=0
         ),
@@ -196,14 +244,14 @@
 
     @pl.when(step == 0)
     def _():
-        rows[...] = got_ref[...].astype(F32)
+        loosen(got_ref, rows)
         held[TOP + 5 * PAIR_ROWS :, :] = jnp.zeros((PACKED - 5 * PAIR_ROWS, K), BF16)
 
     def product(q):
         slot = 2 * pair + q
         values = jnp.concatenate(
             [
-                rows[pl.ds(slot * ROWS + li, WAVES, stride=CHUNK), :]
+                rows[pl.ds(slot * ROWS + li, WAVES, stride=LINE), :]
                 for li in range(ROWS)
             ],
             axis=0,
@@ -233,7 +281,7 @@
         out_specs=pl.BlockSpec((PACKED, K), lambda i: (0, 0)),
         out_shape=jax.ShapeDtypeStruct((PACKED, K), BF16),
         scratch_shapes=[
-            pltpu.VMEM((WAVES * CHUNK, K), F32),
+            pltpu.VMEM((WAVES * LINE, K), F32),
             pltpu.VMEM((TOP + PACKED, K), BF16),
         ],
         compiler_params=params(),
@@ -309,15 +357,14 @@
         back = back * jnp.where(wave == 0, 1.0, 2.0)
         for li in range(ROWS):
             at = (2 * step + q) * ROWS + li
-            rows[pl.ds(at, WAVES, stride=CHUNK), :] = back[li * WAVES : (li + 1) * WAVES]
+            rows[pl.ds(at, WAVES, stride=LINE), :] = back[li * WAVES : (li + 1) * WAVES]
         mine = held[pl.ds(pl.multiple_of(start + begin, UNIT), size), :]
         out_ref[q] = jnp.where(degree >= wave, mine.astype(F32), 0.0).astype(BF16)
 
     @pl.when(step == 4)
     def _():
-        for at in range(SLOTS * ROWS, CHUNK):
-            rows[pl.ds(at, WAVES, stride=CHUNK), :] = jnp.zeros((WAVES, K), F32)
-        send_ref[...] = rows[...].astype(BF16)
+        clear_spare(rows)
+        tighten(rows, send_ref)
 
 
 def inverse(own, block, straight, everything):
@@ -340,7 +387,7 @@
         ],
         scratch_shapes=[
             pltpu.VMEM((TOP + PACKED, K), BF16),
-            pltpu.VMEM((WAVES * CHUNK, K), F32),
+            pltpu.VMEM((WAVES * LINE, K), F32),
         ],
         compiler_params=params(),
         cost_estimate=pl.CostEstimate(
@@ -350,43 +397,63 @@
     )(own, block, straight, everything)
 
 
-def finish_kernel(got_ref, table_ref, out_ref, rows, left):
-    @pl.when(pl.program_id(0) == 0)
-    def _():
-        rows[...] = got_ref[...].astype(F32)
-        for li in range(ROWS):
-            values = jnp.concatenate(
-                [
-                    rows[pl.ds(slot * ROWS + li, WAVES, stride=CHUNK), :]
-                    for slot in range(SLOTS)
-                ],
-                axis=0,
-            )
-            turned = values.T.astype(BF16)
-            at = slice(li * FIELDS, (li + 1) * FIELDS)
-            left[at, :TOP] = turned[:FIELDS]
-            left[at, TOP:] = turned[FIELDS:]
-
-    table = table_ref[...].reshape(2 * TOP, table_ref.shape[2])
-    out_ref[...] = jnp.dot(left[...], table, preferred_element_type=F32).astype(BF16)
+def finish_kernel(got_ref, table_ref, out_ref, table, made, rows, left, loads, stores):
+    parts, _, _, block = table.shape
+
+    def load(part):
+        at = pl.ds(part * block, block)
+        return pltpu.make_async_copy(
+            table_ref.at[:, :, at], table.at[part], loads.at[part]
+        )
+
+    def store(part):
+        at = pl.ds(part * block, block)
+        return pltpu.make_async_copy(made.at[part], out_ref.at[:, at], stores.at[part])
+
+    for part in range(parts):
+        load(part).start()
+    loosen(got_ref, rows)
+    for li in range(ROWS):
+        values = jnp.concatenate(
+            [
+                rows[pl.ds(slot * ROWS + li, WAVES, stride=LINE), :]
+                for slot in range(SLOTS)
+            ],
+            axis=0,
+        )
+        turned = values.T.astype(BF16)
+        at = slice(li * FIELDS, (li + 1) * FIELDS)
+        left[at, :TOP] = turned[:FIELDS]
+        left[at, TOP:] = turned[FIELDS:]
+    for part in range(parts):
+        load(part).wait()
+        right = table[part].reshape(2 * TOP, block)
+        made[part] = jnp.dot(left[...], right, preferred_element_type=F32).astype(BF16)
+        store(part).start()
+    for part in range(parts):
+        store(part).wait()
 
 
 def finish(got, table):
-    block = 512
+    parts = 5
+    block = NLON // parts
     return pl.pallas_call(
         finish_kernel,
-        grid=(NLON // block,),
         in_specs=[
-            pl.BlockSpec((WAVES * CHUNK, K), lambda i: (0, 0)),
-            pl.BlockSpec((2, TOP, block), lambda i: (0, 0, i)),
-        ],
-        out_specs=pl.BlockSpec((ROWS * FIELDS, block), lambda i: (0, i)),
+            pl.BlockSpec(memory_space=pltpu.VMEM),
+            pl.BlockSpec(memory_space=pl.ANY),
+        ],
+        out_specs=pl.BlockSpec(memory_space=pl.ANY),
         out_shape=jax.ShapeDtypeStruct((ROWS * FIELDS, NLON), BF16),
         scratch_shapes=[
-            pltpu.VMEM((WAVES * CHUNK, K), F32),
+            pltpu.VMEM((parts, 2, TOP, block), BF16),
+            pltpu.VMEM((parts, ROWS * FIELDS, block), BF16),
+            pltpu.VMEM((WAVES * LINE, K), F32),
             pltpu.VMEM((ROWS * FIELDS, 2 * TOP), BF16),
-        ],
-        compiler_params=params(),
+            pltpu.SemaphoreType.DMA((parts,)),
+            pltpu.SemaphoreType.DMA((parts,)),
+        ],
+        compiler_params=pltpu.CompilerParams(vmem_limit_bytes=MIDDLE),
         cost_estimate=pl.CostEstimate(
             flops=2 * 192 * 2560 * 1280, bytes_accessed=9000000, transcendentals=0
         ),
@@ -404,7 +471,7 @@
 def body(grid_in, legendre, wave_order, block_order, couple_div, couple_temp):
     lat = lax.axis_index("lat")
     wave = lax.axis_index("wave")
-    send = forward(wave_order.reshape(1, TOP), grid_in.reshape(ROWS * FIELDS, NLON))
+    send = forward(wave_order, grid_in.reshape(ROWS * FIELDS, NLON))
     swap = functools.partial(lax.all_to_all, split_axis=0, concat_axis=0, tiled=True)
     got = swap(send.reshape(WAVES, CHUNK, K), "wave")
     own = lax.dynamic_slice_in_dim(wave_order, wave * SLOTS, SLOTS)

time: 149 us -> 143 us (0.960)
  local copies, waits for them, and re-layouts: 12 us -> 5.23 us
    unnamed x22 -> x16, local copies, waits for them, and re-layouts: 10.1 us -> 3.3 us
    pallas_call x1, Pallas kernels: 5.15 us -> 6.91 us  [inverse_table(): pl.pallas_call(table_kernel, grid=(5,), in_specs=[pl.BlockSpec((128, 128)...]
  transfers between devices with their start and end apart: 3 -> 3, of which waited for: 3 -> 3; matrix products, arithmetic and copies ran while one was open for 1% -> 2% of each run, Pallas kernels for 5% -> 7%
where the time goes in v4:
time: 143 us; the launch traced here: 142 us
  waiting for transfers between devices  62.4 us (44%)
  starting transfers between devices  30.5 us (21%)
  Pallas kernels  29.6 us (21%)
  blocking collectives  13.6 us (10%)
  local copies, waits for them, and re-layouts  5.23 us (4%)
    all_to_all x2, waiting for transfers between devices, body(): got = swap(send.reshape(WAVES, CHUNK, K), 'wave')  49.5 us
    all_to_all x2, starting transfers between devices, body(): got = swap(send.reshape(WAVES, CHUNK, K), 'wave')  25.9 us
    all_gather x1, blocking collectives, body(): everything = lax.all_gather(spectral, 'lat', axis=0, tiled=True)  13.6 us
    all_to_all x1, waiting for transfers between devices, body(): parts = swap(packed.reshape(GROUPS, SHARE, K), 'lat')  12.9 us
    pallas_call x1, Pallas kernels, inverse_table(): pl.pallas_call(table_kernel, grid=(5,), in_specs=[pl.BlockSpec((128, 128)...  6.91 us
    pallas_call x1, Pallas kernels, forward(): pl.pallas_call(forward_kernel, grid=(TOP // 128,), in_specs=[pl.BlockSpec...  6.21 us
    all_to_all x1, starting transfers between devices, body(): parts = swap(packed.reshape(GROUPS, SHARE, K), 'lat')  4.59 us
    pallas_call x1, Pallas kernels, finish(): pl.pallas_call(finish_kernel, in_specs=[pl.BlockSpec(memory_space=pltpu.V...  4.33 us
  transfers between devices with their start and end apart: 3, of which 3 were waited for; matrix products, arithmetic and copies ran while one was open for 2% of the time, Pallas kernels for 7%

profile of v4, /device:TPU:6, one launch (start us, length us, event | category | flops | bytes accessed | tf_op | source)
XLA Modules:
  0.0 142.2 jit_solution(13257407530012884910)
XLA Ops:
  0.6 6.2 %forward_rows.1 = bf16[2048,128]{1,0:T(8,128)(2,1)} custom-call(s32[640]{0:T(1024)} %waves_ref.1, bf16[192,2560]{1,0:T(8,128)(2,1)} %bitcast.18), custom_call_target="tpu_custom_call" | custom-call | flops 1258291200 | bytes 2000000 | tf_op jit(solution)/shard_map/forward_rows/pallas_call | solution.py:145
  6.9 19.0 %all-to-all-start = ((bf16[64,32,128]{2,1,0:T(8,128)(2,1)}), bf16[64,32,128]{2,1,0:T(8,128)(2,1)}, u32[]{:S(2)}, u32[]{:S(2)}) async-start(bf16[64,32,128]{2,1,0:T(8,128)(2,1)} %bitcast.14), calls=%async_computation | async-start | bytes 1048576 | tf_op jit(solution)/shard_map/all_to_all | solution.py:476
  25.9 0.1 dynamic_slice.6.own_ref
  26.0 1.7 %copy-done.2 = bf16[10,192,640]{2,1,0:T(8,128)(2,1)S(1)} copy-done((bf16[10,192,640]{2,1,0:T(8,128)(2,1)S(1)}, bf16[10,192,640]{2,1,0:T(8,128)(2,1)}, u32[]{:S(2)}) %copy-start.2) | copy-done | bytes 2457624
  27.6 2.9 %basis_rows.1 = (bf16[10,192,640]{2,1,0:T(8,128)(2,1)S(1)}, bf16[10,640,192]{2,1,0:T(8,128)(2,1)S(1)}) custom-call(s32[10]{0:T(128)S(1)} %dynamic_slice.6.own_ref, bf16[10,192,640]{2,1,0:T(8,128)(2,1)S(1)} %copy-done.2), custom_call_target="tpu_custom_call" | custom-call | bytes 30000000 | tf_op jit(solution)/shard_map/basis_rows/pallas_call | solution.py:214
  30.6 1.4 %copy-done = bf16[10,192,640]{2,1,0:T(8,128)(2,1)} copy-done((bf16[10,192,640]{2,1,0:T(8,128)(2,1)}, bf16[10,192,640]{2,1,0:T(8,128)(2,1)S(1)}, u32[]{:S(2)}) %copy-start) | copy-done | bytes 2457624
  32.0 25.4 %all-to-all-done = bf16[64,32,128]{2,1,0:T(8,128)(2,1)} async-done(((bf16[64,32,128]{2,1,0:T(8,128)(2,1)}), bf16[64,32,128]{2,1,0:T(8,128)(2,1)}, u32[]{:S(2)}, u32[]{:S(2)}) %all-to-all-start) | async-done | bytes 524320 | tf_op jit(solution)/shard_map/all_to_all | solution.py:476
  57.4 3.9 %partial_sums.1 = bf16[3328,128]{1,0:T(8,128)(2,1)} custom-call(s32[10]{0:T(128)S(1)} %dynamic_slice.6.own_ref, bf16[10,640,192]{2,1,0:T(8,128)(2,1)S(1)} %get-tuple-element.7.turned_ref, bf16[2048,128]{1,0:T(8,128)(2,1)} %bitcast.3.got_ref), custom_call_target="tpu_custom_call" | custom-call | flops 314572800 | bytes 5000000 | tf_op jit(solution)/shard_map/partial_sums/pallas_call | solution.py:273
  61.3 4.6 %all-to-all-start.1 = ((bf16[8,416,128]{2,1,0:T(8,128)(2,1)}), bf16[8,416,128]{2,1,0:T(8,128)(2,1)S(1)}, u32[]{:S(2)}, u32[]{:S(2)}) async-start(bf16[8,416,128]{2,1,0:T(8,128)(2,1)} %bitcast.4), calls=%async_computation.1 | async-start | bytes 1703936 | tf_op jit(solution)/shard_map/all_to_all | solution.py:484
  66.0 0.7 dynamic_slice.7.block_ref
  66.7 0.1 select_maximum_fusion.1
  66.8 0.1 select_maximum_fusion.couple_ref
  66.9 12.9 %all-to-all-done.1.parts_ref = bf16[8,416,128]{2,1,0:T(8,128)(2,1)S(1)} async-done(((bf16[8,416,128]{2,1,0:T(8,128)(2,1)}), bf16[8,416,128]{2,1,0:T(8,128)(2,1)S(1)}, u32[]{:S(2)}, u32[]{:S(2)}) %all-to-all-start.1) | async-done | bytes 852000 | tf_op jit(solution)/shard_map/all_to_all | solution.py:484
  79.7 1.1 couple_levels.1
  80.8 13.6 %all_gather.3.all_ref = bf16[3328,128]{1,0:T(8,128)(2,1)S(1)} all-gather(bf16[416,128]{1,0:T(8,128)(2,1)S(1)} %couple_levels.1), channel_id=1, replica_groups=mesh['lat'=8,'wave'=64] {'lat'}, dimensions={0}, use_global_device_ids=true | all-gather | bytes 958464 | tf_op jit(solution)/shard_map/all_gather | solution.py:486
  94.4 4.3 %inverse_sums.1 = (bf16[10,80,128]{2,1,0:T(8,128)(2,1)}, bf16[2048,128]{1,0:T(8,128)(2,1)}) custom-call(s32[10]{0:T(128)S(1)} %dynamic_slice.6.own_ref, s32[1]{0:T(128)} %dynamic_slice.7.block_ref, bf16[10,192,640]{2,1,0:T(8,128)(2,1)S(1)} %copy-done.1, bf16[3328,128]{1,0:T(8,128)(2,1)S(1)} %all_gather.3.all_ref), custom_call_target="tpu_custom_call" | custom-call | flops 314572800 | bytes 5000000 | tf_op jit(solution)/shard_map/inverse_sums/pallas_call | solution.py:371
  98.7 6.9 %all-to-all-start.2 = ((bf16[64,32,128]{2,1,0:T(8,128)(2,1)}), bf16[64,32,128]{2,1,0:T(8,128)(2,1)S(1)}, u32[]{:S(2)}, u32[]{:S(2)}) async-start(bf16[64,32,128]{2,1,0:T(8,128)(2,1)} %bitcast.8), calls=%async_computation.2 | async-start | bytes 1048576 | tf_op jit(solution)/shard_map/all_to_all | solution.py:488
  105.7 0.1 convert_element_type.18
  105.8 0.1 copy.12
  105.9 0.1 convert_element_type.20
  105.9 0.9 broadcast_in_dim.2.waves_ref
  106.8 6.9 %inverse_table.1.table_ref = bf16[2,640,2560]{2,1,0:T(8,128)(2,1)} custom-call(f32[640,128]{1,0:T(8,128)} %broadcast_in_dim.2.waves_ref), custom_call_target="tpu_custom_call" | custom-call | flops 30000000 | bytes 12000000 | tf_op jit(solution)/shard_map/inverse_table/pallas_call | solution.py:185
  113.8 24.1 %all-to-all-done.2 = bf16[64,32,128]{2,1,0:T(8,128)(2,1)S(1)} async-done(((bf16[64,32,128]{2,1,0:T(8,128)(2,1)}), bf16[64,32,128]{2,1,0:T(8,128)(2,1)S(1)}, u32[]{:S(2)}, u32[]{:S(2)}) %all-to-all-start.2) | async-done | bytes 524320 | tf_op jit(solution)/shard_map/all_to_all | solution.py:488
  137.9 4.3 %finish_rows.1 = bf16[192,2560]{1,0:T(8,128)(2,1)} custom-call(bf16[2048,128]{1,0:T(8,128)(2,1)S(1)} %bitcast.12, bf16[2,640,2560]{2,1,0:T(8,128)(2,1)} %inverse_table.1.table_ref), custom_call_target="tpu_custom_call" | custom-call | flops 1258291200 | bytes 9000000 | tf_op jit(solution)/shard_map/finish_rows/pallas_call | solution.py:440
  (15 shorter events, 0.2 us)
Async XLA Ops:
  0.6 25.2 %copy-start.5 = (s32[640]{0:T(1024)S(1)}, s32[640]{0:T(1024)}, u32[]{:S(2)}) copy-start(s32[640]{0:T(1024)} %waves_ref.1) | copy-start | bytes 7684
  6.9 50.6 %all-to-all-start = ((bf16[64,32,128]{2,1,0:T(8,128)(2,1)}), bf16[64,32,128]{2,1,0:T(8,128)(2,1)}, u32[]{:S(2)}, u32[]{:S(2)}) async-start(bf16[64,32,128]{2,1,0:T(8,128)(2,1)} %bitcast.14), calls=%async_computation | async-start | bytes 1048576 | tf_op jit(solution)/shard_map/all_to_all | solution.py:476
  25.9 1.7 %copy-start.2 = (bf16[10,192,640]{2,1,0:T(8,128)(2,1)S(1)}, bf16[10,192,640]{2,1,0:T(8,128)(2,1)}, u32[]{:S(2)}) copy-start(bf16[10,192,640]{2,1,0:T(8,128)(2,1)} %leg_ref.1) | copy-start | bytes 7372804
  30.6 1.4 %copy-start = (bf16[10,192,640]{2,1,0:T(8,128)(2,1)}, bf16[10,192,640]{2,1,0:T(8,128)(2,1)S(1)}, u32[]{:S(2)}) copy-start(bf16[10,192,640]{2,1,0:T(8,128)(2,1)S(1)} %get-tuple-element.6.straight_ref) | copy-start | bytes 7372804
  32.0 33.9 %copy-start.3 = (f32[32,32]{1,0:T(8,128)S(1)}, f32[32,32]{1,0:T(8,128)}, u32[]{:S(2)}) copy-start(f32[32,32]{1,0:T(8,128)} %param.10) | copy-start | bytes 12292
  32.0 33.9 %copy-start.4 = (f32[32,32]{1,0:T(8,128)S(1)}, f32[32,32]{1,0:T(8,128)}, u32[]{:S(2)}) copy-start(f32[32,32]{1,0:T(8,128)} %param.11) | copy-start | bytes 12292
  32.0 34.0 %copy-start.6 = (s32[8]{0:T(128)S(1)}, s32[8]{0:T(128)}, u32[]{:S(2)}) copy-start(s32[8]{0:T(128)} %param.9) | copy-start | bytes 100
  61.3 33.1 %copy-start.1 = (bf16[10,192,640]{2,1,0:T(8,128)(2,1)S(1)}, bf16[10,192,640]{2,1,0:T(8,128)(2,1)}, u32[]{:S(2)}) copy-start(bf16[10,192,640]{2,1,0:T(8,128)(2,1)} %copy-done) | copy-start | bytes 7372804
  61.3 18.4 %all-to-all-start.1 = ((bf16[8,416,128]{2,1,0:T(8,128)(2,1)}), bf16[8,416,128]{2,1,0:T(8,128)(2,1)S(1)}, u32[]{:S(2)}, u32[]{:S(2)}) async-start(bf16[8,416,128]{2,1,0:T(8,128)(2,1)} %bitcast.4), calls=%async_computation.1 | async-start | bytes 1703936 | tf_op jit(solution)/shard_map/all_to_all | solution.py:484
  98.7 39.2 %all-to-all-start.2 = ((bf16[64,32,128]{2,1,0:T(8,128)(2,1)}), bf16[64,32,128]{2,1,0:T(8,128)(2,1)S(1)}, u32[]{:S(2)}, u32[]{:S(2)}) async-start(bf16[64,32,128]{2,1,0:T(8,128)(2,1)} %bitcast.8), calls=%async_computation.2 | async-start | bytes 1048576 | tf_op jit(solution)/shard_map/all_to_all | solution.py:488

commit v5 on v4

--- a/solution.py
+++ b/solution.py
@@ -11,6 +11,7 @@
 F32 = jnp.float32
 BF16 = jnp.bfloat16
 NLON = 2560
+HALF = NLON // 2
 WAVES = 64
 GROUPS = 8
 SLOTS = 10
@@ -28,7 +29,7 @@
 SHARE = PACKED // GROUPS
 VMEM_LIMIT = 24 * 1024 * 1024
 LARGE = 58 * 1024 * 1024
-MIDDLE = 50 * 1024 * 1024
+MIDDLE = 52 * 1024 * 1024
 
 
 def params(limit=VMEM_LIMIT):
@@ -64,49 +65,51 @@
     return product - NLON * jnp.floor((product + 0.5) * (1.0 / NLON))
 
 
-def forward_kernel(waves_ref, grid_ref, send_ref, grid, lines, rows, sem):
+def forward_kernel(waves_ref, grid_ref, send_ref, grid, near, far, lines, rows, sem):
     step = pl.program_id(0)
-    load = pltpu.make_async_copy(grid_ref, grid, sem)
 
     @pl.when(step == 0)
     def _():
+        load = pltpu.make_async_copy(grid_ref, grid, sem)
         load.start()
-
-    waves = jnp.zeros((1, 128), F32)
-    for part in range(TOP // 128):
-        one = waves_ref[part * 128 : (part + 1) * 128].astype(F32).reshape(1, 128)
-        waves = jnp.where(step == part, one, waves)
-    down = lax.broadcasted_iota(jnp.int32, (128, 128), 0).astype(F32)
-    near_c, near_s = cos_sin(phase_of(waves * down))
-    far_c, far_s = cos_sin(phase_of(waves * (down[:16] * 128.0)))
-    factor = 1.0 / math.sqrt(NLON)
-    far_c = far_c * factor
-    far_s = far_s * factor
-    sign = 1.0 - 2.0 * (waves - 2.0 * jnp.floor(waves * 0.5))
-
-    @pl.when(step == 0)
-    def _():
+        waves = waves_ref[...].astype(F32).reshape(1, TOP)
+        down = lax.broadcasted_iota(jnp.int32, (128, TOP), 0).astype(F32)
+        c, s = cos_sin(phase_of(waves * down))
+        near[0] = c
+        near[1] = s
+        c, s = cos_sin(phase_of(waves * (down[:16] * 128.0)))
+        factor = 1.0 / math.sqrt(NLON)
+        far[0] = c * factor
+        far[1] = s * factor
         load.wait()
 
-    made = jnp.zeros((ROWS * FIELDS, 256), F32)
-    half = NLON // 2
-    for a in range(half // 128):
-        ca = far_c[a : a + 1]
-        sa = far_s[a : a + 1]
-        c = ca * near_c - sa * near_s
-        s = -(sa * near_c) - ca * near_s
-        first = jnp.concatenate([c, s], axis=1).astype(BF16)
-        second = jnp.concatenate([c * sign, s * sign], axis=1).astype(BF16)
+    at = pl.ds(pl.multiple_of(step * 128, 128), 128)
+    near_c = near[0, :, at]
+    near_s = near[1, :, at]
+    far_c = far[0, :, at]
+    far_s = far[1, :, at]
+    made = jnp.zeros((2 * ROWS * FIELDS, 256), F32)
+    for a in range(0, HALF // 128, 2):
+        right = []
+        for b in (a, a + 1):
+            ca = far_c[b : b + 1]
+            sa = far_s[b : b + 1]
+            c = ca * near_c - sa * near_s
+            s = -(sa * near_c) - ca * near_s
+            right.append(jnp.concatenate([c, s], axis=1).astype(BF16))
         left = jnp.concatenate(
             [
-                grid[:, a * 128 : (a + 1) * 128],
-                grid[:, half + a * 128 : half + (a + 1) * 128],
+                grid[:, a * 128 : (a + 2) * 128],
+                grid[:, HALF + a * 128 : HALF + (a + 2) * 128],
             ],
-            axis=1,
+            axis=0,
         )
-        right = jnp.concatenate([first, second], axis=0)
-        made = made + jnp.dot(left, right, preferred_element_type=F32)
-    at = pl.ds(pl.multiple_of(step * 128, 128), 128)
+        made = made + jnp.dot(
+            left, jnp.concatenate(right, axis=0), preferred_element_type=F32
+        )
+    sign = jnp.where(far_c[HALF // 128 : HALF // 128 + 1] > 0.0, 1.0, -1.0)
+    sign = jnp.concatenate([sign, sign], axis=1)
+    made = made[: ROWS * FIELDS] + sign * made[ROWS * FIELDS :]
     for li in range(ROWS):
         one = made[li * FIELDS : (li + 1) * FIELDS]
         lines[li, at, :] = jnp.concatenate([one[:, :128], one[:, 128:]], axis=0).T
@@ -153,6 +156,8 @@
         out_shape=jax.ShapeDtypeStruct((WAVES * CHUNK, K), BF16),
         scratch_shapes=[
             pltpu.VMEM((ROWS * FIELDS, NLON), BF16),
+            pltpu.VMEM((2, 128, TOP), F32),
+            pltpu.VMEM((2, 16, TOP), F32),
             pltpu.VMEM((ROWS, TOP, K), F32),
             pltpu.VMEM((WAVES * LINE, K), F32),
             pltpu.SemaphoreType.DMA,
@@ -173,7 +178,7 @@
     factor = 1.0 / math.sqrt(NLON)
     far_c = far_c * factor
     far_s = far_s * factor
-    for a in range(NLON // 128):
+    for a in range(HALF // 128):
         ca = far_c[:, a : a + 1]
         sa = far_s[:, a : a + 1]
         at = slice(a * 128, (a + 1) * 128)
@@ -186,11 +191,11 @@
         table_kernel,
         grid=(5,),
         in_specs=[pl.BlockSpec((128, 128), lambda i: (i, 0))],
-        out_specs=pl.BlockSpec((2, 128, NLON), lambda i: (0, i, 0)),
-        out_shape=jax.ShapeDtypeStruct((2, TOP, NLON), BF16),
+        out_specs=pl.BlockSpec((2, 128, HALF), lambda i: (0, i, 0)),
+        out_shape=jax.ShapeDtypeStruct((2, TOP, HALF), BF16),
         compiler_params=params(LARGE),
         cost_estimate=pl.CostEstimate(
-            flops=30000000, bytes_accessed=12000000, transcendentals=0
+            flops=30000000, bytes_accessed=6000000, transcendentals=0
         ),
         name="inverse_table",
     )(waves)
@@ -397,22 +402,28 @@
     )(own, block, straight, everything)
 
 
-def finish_kernel(got_ref, table_ref, out_ref, table, made, rows, left, loads, stores):
+def finish_kernel(
+    got_ref, sign_ref, table_ref, out_ref, table, made, rows, left, loads, stores
+):
     parts, _, _, block = table.shape
+    lines = ROWS * FIELDS
 
     def load(part):
-        at = pl.ds(part * block, block)
+        at = pl.ds(pl.multiple_of(part * block, 128), block)
         return pltpu.make_async_copy(
             table_ref.at[:, :, at], table.at[part], loads.at[part]
         )
 
-    def store(part):
-        at = pl.ds(part * block, block)
-        return pltpu.make_async_copy(made.at[part], out_ref.at[:, at], stores.at[part])
+    def store(part, half):
+        at = pl.ds(pl.multiple_of(half * HALF + part * block, 128), block)
+        return pltpu.make_async_copy(
+            made.at[part, half], out_ref.at[:, at], stores.at[part, half]
+        )
 
     for part in range(parts):
         load(part).start()
     loosen(got_ref, rows)
+    sign = sign_ref[...]
     for li in range(ROWS):
         values = jnp.concatenate(
             [
@@ -421,25 +432,32 @@
             ],
             axis=0,
         )
-        turned = values.T.astype(BF16)
-        at = slice(li * FIELDS, (li + 1) * FIELDS)
-        left[at, :TOP] = turned[:FIELDS]
-        left[at, TOP:] = turned[FIELDS:]
-    for part in range(parts):
+        turned = values.T
+        for half, one in enumerate((turned, turned * sign)):
+            at = slice(half * lines + li * FIELDS, half * lines + (li + 1) * FIELDS)
+            left[at, :TOP] = one[:FIELDS].astype(BF16)
+            left[at, TOP:] = one[FIELDS:].astype(BF16)
+
+    @pl.loop(0, parts)
+    def _(part):
         load(part).wait()
         right = table[part].reshape(2 * TOP, block)
-        made[part] = jnp.dot(left[...], right, preferred_element_type=F32).astype(BF16)
-        store(part).start()
+        both = jnp.dot(left[...], right, preferred_element_type=F32).astype(BF16)
+        for half in range(2):
+            made[part, half] = both[half * lines : (half + 1) * lines]
+            store(part, half).start()
     for part in range(parts):
-        store(part).wait()
-
-
-def finish(got, table):
+        for half in range(2):
+            store(part, half).wait()
+
+
+def finish(got, sign, table):
     parts = 5
-    block = NLON // parts
+    block = HALF // parts
     return pl.pallas_call(
         finish_kernel,
         in_specs=[
+            pl.BlockSpec(memory_space=pltpu.VMEM),
             pl.BlockSpec(memory_space=pltpu.VMEM),
             pl.BlockSpec(memory_space=pl.ANY),
         ],
@@ -447,18 +465,18 @@
         out_shape=jax.ShapeDtypeStruct((ROWS * FIELDS, NLON), BF16),
         scratch_shapes=[
             pltpu.VMEM((parts, 2, TOP, block), BF16),
-            pltpu.VMEM((parts, ROWS * FIELDS, block), BF16),
+            pltpu.VMEM((parts, 2, ROWS * FIELDS, block), BF16),
             pltpu.VMEM((WAVES * LINE, K), F32),
-            pltpu.VMEM((ROWS * FIELDS, 2 * TOP), BF16),
+            pltpu.VMEM((2 * ROWS * FIELDS, 2 * TOP), BF16),
             pltpu.SemaphoreType.DMA((parts,)),
-            pltpu.SemaphoreType.DMA((parts,)),
+            pltpu.SemaphoreType.DMA((parts, 2)),
         ],
         compiler_params=pltpu.CompilerParams(vmem_limit_bytes=MIDDLE),
         cost_estimate=pl.CostEstimate(
-            flops=2 * 192 * 2560 * 1280, bytes_accessed=9000000, transcendentals=0
+            flops=2 * 192 * 2560 * 1280, bytes_accessed=6000000, transcendentals=0
         ),
         name="finish_rows",
-    )(got, table)
+    )(got, sign, table)
 
 
 def coupling_matrix(couple_div, couple_temp):
@@ -477,8 +495,9 @@
     own = lax.dynamic_slice_in_dim(wave_order, wave * SLOTS, SLOTS)
     block = lax.dynamic_slice_in_dim(block_order, lat, 1)
     straight, turned = basis(own, legendre)
-    waves = wave_order.reshape(WAVES, SLOTS).T.reshape(TOP, 1).astype(F32)
-    table = inverse_table(jnp.broadcast_to(waves, (TOP, 128)))
+    waves = wave_order.reshape(WAVES, SLOTS).T.reshape(TOP)
+    sign = (1 - 2 * (waves & 1)).astype(F32).reshape(1, TOP)
+    table = inverse_table(jnp.broadcast_to(waves.astype(F32)[:, None], (TOP, 128)))
     matrix = coupling_matrix(couple_div, couple_temp)
     packed = partial_sums(own, turned, got.reshape(WAVES * CHUNK, K))
     parts = swap(packed.reshape(GROUPS, SHARE, K), "lat")
@@ -486,7 +505,7 @@
     everything = lax.all_gather(spectral, "lat", axis=0, tiled=True)
     spectral_out, send = inverse(own, block, straight, everything)
     got = swap(send.reshape(WAVES, CHUNK, K), "wave")
-    grid_out = finish(got.reshape(WAVES * CHUNK, K), table)
+    grid_out = finish(got.reshape(WAVES * CHUNK, K), sign, table)
     return spectral_out.transpose(1, 0, 2), grid_out.reshape(ROWS, FIELDS, NLON)
 
 

time: 143 us -> 142 us (level)
  Pallas kernels: 29.6 us -> 27.2 us
    pallas_call x1, Pallas kernels: 6.91 us -> 5.31 us  [inverse_table(): pl.pallas_call(table_kernel, grid=(5,), in_specs=[pl.BlockSpec((128, 128)...]
  transfers between devices with their start and end apart: 3 -> 3, of which waited for: 3 -> 3; matrix products, arithmetic and copies ran while one was open for 2% -> 2% of each run, Pallas kernels for 7% -> 6%
where the time goes in v5:
time: 142 us; the launch traced here: 141 us
  waiting for transfers between devices  63.7 us (45%)
  starting transfers between devices  30.5 us (21%)
  Pallas kernels  27.2 us (19%)
  blocking collectives  13.6 us (10%)
  local copies, waits for them, and re-layouts  5.52 us (4%)
    all_to_all x2, waiting for transfers between devices, body(): got = swap(send.reshape(WAVES, CHUNK, K), 'wave')  50.8 us
    all_to_all x2, starting transfers between devices, body(): got = swap(send.reshape(WAVES, CHUNK, K), 'wave')  25.9 us
    all_gather x1, blocking collectives, body(): everything = lax.all_gather(spectral, 'lat', axis=0, tiled=True)  13.6 us
    all_to_all x1, waiting for transfers between devices, body(): parts = swap(packed.reshape(GROUPS, SHARE, K), 'lat')  12.9 us
    pallas_call x1, Pallas kernels, forward(): pl.pallas_call(forward_kernel, grid=(TOP // 128,), in_specs=[pl.BlockSpec...  5.7 us
    pallas_call x1, Pallas kernels, inverse_table(): pl.pallas_call(table_kernel, grid=(5,), in_specs=[pl.BlockSpec((128, 128)...  5.31 us
    all_to_all x1, starting transfers between devices, body(): parts = swap(packed.reshape(GROUPS, SHARE, K), 'lat')  4.62 us
    pallas_call x1, Pallas kernels, inverse(): pl.pallas_call(inverse_kernel, grid=(5,), in_specs=[pl.BlockSpec(memory_s...  4.25 us
  transfers between devices with their start and end apart: 3, of which 3 were waited for; matrix products, arithmetic and copies ran while one was open for 2% of the time, Pallas kernels for 6%

profile of v5, /device:TPU:6, one launch (start us, length us, event | category | flops | bytes accessed | tf_op | source)
XLA Modules:
  0.0 141.4 jit_solution(8777772404754035247)
XLA Ops:
  0.6 5.7 %forward_rows.1 = bf16[2048,128]{1,0:T(8,128)(2,1)} custom-call(s32[640]{0:T(1024)} %waves_ref.1, bf16[192,2560]{1,0:T(8,128)(2,1)} %bitcast.20), custom_call_target="tpu_custom_call" | custom-call | flops 1258291200 | bytes 2000000 | tf_op jit(solution)/shard_map/forward_rows/pallas_call | solution.py:148
  6.3 19.0 %all-to-all-start = ((bf16[64,32,128]{2,1,0:T(8,128)(2,1)}), bf16[64,32,128]{2,1,0:T(8,128)(2,1)}, u32[]{:S(2)}, u32[]{:S(2)}) async-start(bf16[64,32,128]{2,1,0:T(8,128)(2,1)} %bitcast.15), calls=%async_computation | async-start | bytes 1048576 | tf_op jit(solution)/shard_map/all_to_all | solution.py:494
  25.4 0.1 dynamic_slice.6.own_ref
  25.4 1.7 %copy-done.2 = bf16[10,192,640]{2,1,0:T(8,128)(2,1)S(1)} copy-done((bf16[10,192,640]{2,1,0:T(8,128)(2,1)S(1)}, bf16[10,192,640]{2,1,0:T(8,128)(2,1)}, u32[]{:S(2)}) %copy-start.2) | copy-done | bytes 2457624
  27.1 2.9 %basis_rows.1 = (bf16[10,192,640]{2,1,0:T(8,128)(2,1)S(1)}, bf16[10,640,192]{2,1,0:T(8,128)(2,1)S(1)}) custom-call(s32[10]{0:T(128)S(1)} %dynamic_slice.6.own_ref, bf16[10,192,640]{2,1,0:T(8,128)(2,1)S(1)} %copy-done.2), custom_call_target="tpu_custom_call" | custom-call | bytes 30000000 | tf_op jit(solution)/shard_map/basis_rows/pallas_call | solution.py:219
  30.1 1.5 %copy-done = bf16[10,192,640]{2,1,0:T(8,128)(2,1)} copy-done((bf16[10,192,640]{2,1,0:T(8,128)(2,1)}, bf16[10,192,640]{2,1,0:T(8,128)(2,1)S(1)}, u32[]{:S(2)}) %copy-start) | copy-done | bytes 2457624
  31.5 25.4 %all-to-all-done = bf16[64,32,128]{2,1,0:T(8,128)(2,1)} async-done(((bf16[64,32,128]{2,1,0:T(8,128)(2,1)}), bf16[64,32,128]{2,1,0:T(8,128)(2,1)}, u32[]{:S(2)}, u32[]{:S(2)}) %all-to-all-start) | async-done | bytes 524320 | tf_op jit(solution)/shard_map/all_to_all | solution.py:494
  56.9 3.9 %partial_sums.1 = bf16[3328,128]{1,0:T(8,128)(2,1)} custom-call(s32[10]{0:T(128)S(1)} %dynamic_slice.6.own_ref, bf16[10,640,192]{2,1,0:T(8,128)(2,1)S(1)} %get-tuple-element.7.turned_ref, bf16[2048,128]{1,0:T(8,128)(2,1)} %bitcast.3.got_ref), custom_call_target="tpu_custom_call" | custom-call | flops 314572800 | bytes 5000000 | tf_op jit(solution)/shard_map/partial_sums/pallas_call | solution.py:278
  60.8 4.6 %all-to-all-start.1 = ((bf16[8,416,128]{2,1,0:T(8,128)(2,1)}), bf16[8,416,128]{2,1,0:T(8,128)(2,1)S(1)}, u32[]{:S(2)}, u32[]{:S(2)}) async-start(bf16[8,416,128]{2,1,0:T(8,128)(2,1)} %bitcast.4), calls=%async_computation.1 | async-start | bytes 1703936 | tf_op jit(solution)/shard_map/all_to_all | solution.py:503
  65.6 0.7 dynamic_slice.7.block_ref
  66.2 0.1 select_maximum_fusion.1
  66.3 0.1 select_maximum_fusion.couple_ref
  66.4 12.9 %all-to-all-done.1.parts_ref = bf16[8,416,128]{2,1,0:T(8,128)(2,1)S(1)} async-done(((bf16[8,416,128]{2,1,0:T(8,128)(2,1)}), bf16[8,416,128]{2,1,0:T(8,128)(2,1)S(1)}, u32[]{:S(2)}, u32[]{:S(2)}) %all-to-all-start.1) | async-done | bytes 852000 | tf_op jit(solution)/shard_map/all_to_all | solution.py:503
  79.3 1.1 couple_levels.1
  80.3 13.6 %all_gather.3.all_ref = bf16[3328,128]{1,0:T(8,128)(2,1)S(1)} all-gather(bf16[416,128]{1,0:T(8,128)(2,1)S(1)} %couple_levels.1), channel_id=1, replica_groups=mesh['lat'=8,'wave'=64] {'lat'}, dimensions={0}, use_global_device_ids=true | all-gather | bytes 958464 | tf_op jit(solution)/shard_map/all_gather | solution.py:505
  93.9 4.3 %inverse_sums.1 = (bf16[10,80,128]{2,1,0:T(8,128)(2,1)}, bf16[2048,128]{1,0:T(8,128)(2,1)}) custom-call(s32[10]{0:T(128)S(1)} %dynamic_slice.6.own_ref, s32[1]{0:T(128)} %dynamic_slice.7.block_ref, bf16[10,192,640]{2,1,0:T(8,128)(2,1)S(1)} %copy-done.1, bf16[3328,128]{1,0:T(8,128)(2,1)S(1)} %all_gather.3.all_ref), custom_call_target="tpu_custom_call" | custom-call | flops 314572800 | bytes 5000000 | tf_op jit(solution)/shard_map/inverse_sums/pallas_call | solution.py:376
  98.2 6.9 %all-to-all-start.2 = ((bf16[64,32,128]{2,1,0:T(8,128)(2,1)}), bf16[64,32,128]{2,1,0:T(8,128)(2,1)S(1)}, u32[]{:S(2)}, u32[]{:S(2)}) async-start(bf16[64,32,128]{2,1,0:T(8,128)(2,1)} %bitcast.8), calls=%async_computation.2 | async-start | bytes 1048576 | tf_op jit(solution)/shard_map/all_to_all | solution.py:507
  105.1 0.1 convert_element_type.32
  105.4 0.1 reshape.78
  105.6 0.1 convert_element_type.30.sign_ref
  105.7 0.9 broadcast_in_dim.2.waves_ref
  106.6 5.3 %inverse_table.1.table_ref = bf16[2,640,1280]{2,1,0:T(8,128)(2,1)} custom-call(f32[640,128]{1,0:T(8,128)} %broadcast_in_dim.2.waves_ref), custom_call_target="tpu_custom_call" | custom-call | flops 30000000 | bytes 6000000 | tf_op jit(solution)/shard_map/inverse_table/pallas_call | solution.py:190
  111.9 25.4 %all-to-all-done.2 = bf16[64,32,128]{2,1,0:T(8,128)(2,1)S(1)} async-done(((bf16[64,32,128]{2,1,0:T(8,128)(2,1)}), bf16[64,32,128]{2,1,0:T(8,128)(2,1)S(1)}, u32[]{:S(2)}, u32[]{:S(2)}) %all-to-all-start.2) | async-done | bytes 524320 | tf_op jit(solution)/shard_map/all_to_all | solution.py:507
  137.3 4.0 %finish_rows.1 = bf16[192,2560]{1,0:T(8,128)(2,1)} custom-call(bf16[2048,128]{1,0:T(8,128)(2,1)S(1)} %bitcast.13, f32[1,640]{1,0:T(1,128)S(1)} %convert_element_type.30.sign_ref, bf16[2,640,1280]{2,1,0:T(8,128)(2,1)} %inverse_table.1.table_ref), custom_call_target="tpu_custom_call" | custom-call | flops 1258291200 | bytes 6000000 | tf_op jit(solution)/shard_map/finish_rows/pallas_call | solution.py:457
  (18 shorter events, 0.4 us)
Async XLA Ops:
  0.6 24.7 %copy-start.5 = (s32[640]{0:T(1024)S(1)}, s32[640]{0:T(1024)}, u32[]{:S(2)}) copy-start(s32[640]{0:T(1024)} %waves_ref.1) | copy-start | bytes 7684
  6.3 50.6 %all-to-all-start = ((bf16[64,32,128]{2,1,0:T(8,128)(2,1)}), bf16[64,32,128]{2,1,0:T(8,128)(2,1)}, u32[]{:S(2)}, u32[]{:S(2)}) async-start(bf16[64,32,128]{2,1,0:T(8,128)(2,1)} %bitcast.15), calls=%async_computation | async-start | bytes 1048576 | tf_op jit(solution)/shard_map/all_to_all | solution.py:494
  25.4 1.7 %copy-start.2 = (bf16[10,192,640]{2,1,0:T(8,128)(2,1)S(1)}, bf16[10,192,640]{2,1,0:T(8,128)(2,1)}, u32[]{:S(2)}) copy-start(bf16[10,192,640]{2,1,0:T(8,128)(2,1)} %leg_ref.1) | copy-start | bytes 7372804
  30.1 1.5 %copy-start = (bf16[10,192,640]{2,1,0:T(8,128)(2,1)}, bf16[10,192,640]{2,1,0:T(8,128)(2,1)S(1)}, u32[]{:S(2)}) copy-start(bf16[10,192,640]{2,1,0:T(8,128)(2,1)S(1)} %get-tuple-element.6.straight_ref) | copy-start | bytes 7372804
  31.5 33.9 %copy-start.3 = (f32[32,32]{1,0:T(8,128)S(1)}, f32[32,32]{1,0:T(8,128)}, u32[]{:S(2)}) copy-start(f32[32,32]{1,0:T(8,128)} %param.11) | copy-start | bytes 12292
  31.5 34.0 %copy-start.4 = (f32[32,32]{1,0:T(8,128)S(1)}, f32[32,32]{1,0:T(8,128)}, u32[]{:S(2)}) copy-start(f32[32,32]{1,0:T(8,128)} %param.10) | copy-start | bytes 12292
  31.5 34.0 %copy-start.6 = (s32[8]{0:T(128)S(1)}, s32[8]{0:T(128)}, u32[]{:S(2)}) copy-start(s32[8]{0:T(128)} %param.9) | copy-start | bytes 100
  60.8 33.2 %copy-start.1 = (bf16[10,192,640]{2,1,0:T(8,128)(2,1)S(1)}, bf16[10,192,640]{2,1,0:T(8,128)(2,1)}, u32[]{:S(2)}) copy-start(bf16[10,192,640]{2,1,0:T(8,128)(2,1)} %copy-done) | copy-start | bytes 7372804
  60.8 18.5 %all-to-all-start.1 = ((bf16[8,416,128]{2,1,0:T(8,128)(2,1)}), bf16[8,416,128]{2,1,0:T(8,128)(2,1)S(1)}, u32[]{:S(2)}, u32[]{:S(2)}) async-start(bf16[8,416,128]{2,1,0:T(8,128)(2,1)} %bitcast.4), calls=%async_computation.1 | async-start | bytes 1703936 | tf_op jit(solution)/shard_map/all_to_all | solution.py:503
  98.2 39.1 %all-to-all-start.2 = ((bf16[64,32,128]{2,1,0:T(8,128)(2,1)}), bf16[64,32,128]{2,1,0:T(8,128)(2,1)S(1)}, u32[]{:S(2)}, u32[]{:S(2)}) async-start(bf16[64,32,128]{2,1,0:T(8,128)(2,1)} %bitcast.8), calls=%async_computation.2 | async-start | bytes 1048576 | tf_op jit(solution)/shard_map/all_to_all | solution.py:507

commit v6 on v5

--- a/solution.py
+++ b/solution.py
@@ -70,8 +70,16 @@
 
     @pl.when(step == 0)
     def _():
-        load = pltpu.make_async_copy(grid_ref, grid, sem)
-        load.start()
+        loads = [
+            pltpu.make_async_copy(
+                grid_ref.at[:, pl.ds(half * HALF, HALF)],
+                grid.at[pl.ds(half * ROWS * FIELDS, ROWS * FIELDS)],
+                sem.at[half],
+            )
+            for half in range(2)
+        ]
+        for load in loads:
+            load.start()
         waves = waves_ref[...].astype(F32).reshape(1, TOP)
         down = lax.broadcasted_iota(jnp.int32, (128, TOP), 0).astype(F32)
         c, s = cos_sin(phase_of(waves * down))
@@ -81,7 +89,8 @@
         factor = 1.0 / math.sqrt(NLON)
         far[0] = c * factor
         far[1] = s * factor
-        load.wait()
+        for load in loads:
+            load.wait()
 
     at = pl.ds(pl.multiple_of(step * 128, 128), 128)
     near_c = near[0, :, at]
@@ -97,15 +106,10 @@
             c = ca * near_c - sa * near_s
             s = -(sa * near_c) - ca * near_s
             right.append(jnp.concatenate([c, s], axis=1).astype(BF16))
-        left = jnp.concatenate(
-            [
-                grid[:, a * 128 : (a + 2) * 128],
-                grid[:, HALF + a * 128 : HALF + (a + 2) * 128],
-            ],
-            axis=0,
-        )
         made = made + jnp.dot(
-            left, jnp.concatenate(right, axis=0), preferred_element_type=F32
+            grid[:, a * 128 : (a + 2) * 128],
+            jnp.concatenate(right, axis=0),
+            preferred_element_type=F32,
         )
     sign = jnp.where(far_c[HALF // 128 : HALF // 128 + 1] > 0.0, 1.0, -1.0)
     sign = jnp.concatenate([sign, sign], axis=1)
@@ -155,12 +159,12 @@
         out_specs=pl.BlockSpec((WAVES * CHUNK, K), lambda i: (0, 0)),
         out_shape=jax.ShapeDtypeStruct((WAVES * CHUNK, K), BF16),
         scratch_shapes=[
-            pltpu.VMEM((ROWS * FIELDS, NLON), BF16),
+            pltpu.VMEM((2 * ROWS * FIELDS, HALF), BF16),
             pltpu.VMEM((2, 128, TOP), F32),
             pltpu.VMEM((2, 16, TOP), F32),
             pltpu.VMEM((ROWS, TOP, K), F32),
             pltpu.VMEM((WAVES * LINE, K), F32),
-            pltpu.SemaphoreType.DMA,
+            pltpu.SemaphoreType.DMA((2,)),
         ],
         compiler_params=params(LARGE),
         cost_estimate=pl.CostEstimate(
@@ -499,9 +503,12 @@
     sign = (1 - 2 * (waves & 1)).astype(F32).reshape(1, TOP)
     table = inverse_table(jnp.broadcast_to(waves.astype(F32)[:, None], (TOP, 128)))
     matrix = coupling_matrix(couple_div, couple_temp)
+    turned, straight, table, sign, matrix, block, own, lat = lax.optimization_barrier(
+        (turned, straight, table, sign, matrix, block, own, lat.reshape(1))
+    )
     packed = partial_sums(own, turned, got.reshape(WAVES * CHUNK, K))
     parts = swap(packed.reshape(GROUPS, SHARE, K), "lat")
-    spectral = couple(own, lat.reshape(1), parts, matrix)
+    spectral = couple(own, lat, parts, matrix)
     everything = lax.all_gather(spectral, "lat", axis=0, tiled=True)
     spectral_out, send = inverse(own, block, straight, everything)
     got = swap(send.reshape(WAVES, CHUNK, K), "wave")

time: 142 us -> 141 us (level)
  blocking collectives: 13.6 us -> 70.7 us
  waiting for transfers between devices: 63.7 us -> 17.7 us
  starting transfers between devices: 30.5 us -> 19 us
    all_to_all x0 -> x2, blocking collectives: none -> 57.2 us  [the longest x1 38.9 us: body(): got = swap(send.reshape(WAVES, CHUNK, K), 'wave')]
    all_to_all x2 -> x1, waiting for transfers between devices: 50.8 us -> 17.7 us  [body(): got = swap(send.reshape(WAVES, CHUNK, K), 'wave')]
    all_to_all x1 -> x0, waiting for transfers between devices: 12.9 us -> none  [body(): parts = swap(packed.reshape(GROUPS, SHARE, K), 'lat')]
    all_to_all x2 -> x1, starting transfers between devices: 25.9 us -> 19 us  [body(): got = swap(send.reshape(WAVES, CHUNK, K), 'wave')]
    all_to_all x1 -> x0, starting transfers between devices: 4.62 us -> none  [body(): parts = swap(packed.reshape(GROUPS, SHARE, K), 'lat')]
  transfers between devices with their start and end apart: 3 -> 1, of which waited for: 3 -> 1; matrix products, arithmetic and copies ran while one was open for 2% -> 2% of each run, Pallas kernels for 6% -> 6%
where the time goes in v6:
time: 141 us; the launch traced here: 140 us
  blocking collectives  70.7 us (50%)
  Pallas kernels  26.2 us (19%)
  starting transfers between devices  19 us (13%)
  waiting for transfers between devices  17.7 us (13%)
  local copies, waits for them, and re-layouts  5.47 us (4%)
    all_to_all x1, blocking collectives, body(): got = swap(send.reshape(WAVES, CHUNK, K), 'wave')  38.9 us
    all_to_all x1, starting transfers between devices, body(): got = swap(send.reshape(WAVES, CHUNK, K), 'wave')  19 us
    all_to_all x1, blocking collectives, body(): parts = swap(packed.reshape(GROUPS, SHARE, K), 'lat')  18.2 us
    all_to_all x1, waiting for transfers between devices, body(): got = swap(send.reshape(WAVES, CHUNK, K), 'wave')  17.7 us
    all_gather x1, blocking collectives, body(): everything = lax.all_gather(spectral, 'lat', axis=0, tiled=True)  13.6 us
    pallas_call x1, Pallas kernels, forward(): pl.pallas_call(forward_kernel, grid=(TOP // 128,), in_specs=[pl.BlockSpec...  5.65 us
    pallas_call x1, Pallas kernels, inverse_table(): pl.pallas_call(table_kernel, grid=(5,), in_specs=[pl.BlockSpec((128, 128)...  5.33 us
    pallas_call x1, Pallas kernels, inverse(): pl.pallas_call(inverse_kernel, grid=(5,), in_specs=[pl.BlockSpec(memory_s...  4.05 us
  transfers between devices with their start and end apart: 1, of which 1 were waited for; matrix products, arithmetic and copies ran while one was open for 2% of the time, Pallas kernels for 6%

profile of v6, /device:TPU:6, one launch (start us, length us, event | category | flops | bytes accessed | tf_op | source)
XLA Modules:
  0.0 139.9 jit_solution(9107403827405451375)
XLA Ops:
  0.7 5.6 %forward_rows.1 = bf16[2048,128]{1,0:T(8,128)(2,1)} custom-call(s32[640]{0:T(1024)} %waves_ref.1, bf16[192,2560]{1,0:T(8,128)(2,1)} %bitcast.22), custom_call_target="tpu_custom_call" | custom-call | flops 1258291200 | bytes 2000000 | tf_op jit(solution)/shard_map/forward_rows/pallas_call | solution.py:152
  6.3 19.0 %all-to-all-start = ((bf16[64,32,128]{2,1,0:T(8,128)(2,1)}), bf16[64,32,128]{2,1,0:T(8,128)(2,1)}, u32[]{:S(2)}, u32[]{:S(2)}) async-start(bf16[64,32,128]{2,1,0:T(8,128)(2,1)} %bitcast.17), calls=%async_computation | async-start | bytes 1048576 | tf_op jit(solution)/shard_map/all_to_all | solution.py:498
  25.3 0.1 dynamic_slice.6.own_ref
  25.6 0.1 reshape.78
  25.7 0.1 copy.11
  25.8 0.1 convert_element_type.34.sign_ref
  25.9 0.1 convert_element_type.30
  26.0 0.1 copy.10
  26.2 0.6 dynamic_slice.7.block_ref
  26.8 1.7 %copy-done.2 = bf16[10,192,640]{2,1,0:T(8,128)(2,1)S(1)} copy-done((bf16[10,192,640]{2,1,0:T(8,128)(2,1)S(1)}, bf16[10,192,640]{2,1,0:T(8,128)(2,1)}, u32[]{:S(2)}) %copy-start.2) | copy-done | bytes 2457624
  28.5 2.9 %basis_rows.1 = (bf16[10,192,640]{2,1,0:T(8,128)(2,1)S(1)}, bf16[10,640,192]{2,1,0:T(8,128)(2,1)S(1)}) custom-call(s32[10]{0:T(128)S(1)} %dynamic_slice.6.own_ref, bf16[10,192,640]{2,1,0:T(8,128)(2,1)S(1)} %copy-done.2), custom_call_target="tpu_custom_call" | custom-call | bytes 30000000 | tf_op jit(solution)/shard_map/basis_rows/pallas_call | solution.py:223
  31.4 1.5 %copy-done = bf16[10,192,640]{2,1,0:T(8,128)(2,1)} copy-done((bf16[10,192,640]{2,1,0:T(8,128)(2,1)}, bf16[10,192,640]{2,1,0:T(8,128)(2,1)S(1)}, u32[]{:S(2)}) %copy-start) | copy-done | bytes 2457624
  32.9 0.9 broadcast_in_dim.2.waves_ref
  33.8 5.3 %inverse_table.1.table_ref = bf16[2,640,1280]{2,1,0:T(8,128)(2,1)} custom-call(f32[640,128]{1,0:T(8,128)} %broadcast_in_dim.2.waves_ref), custom_call_target="tpu_custom_call" | custom-call | flops 30000000 | bytes 6000000 | tf_op jit(solution)/shard_map/inverse_table/pallas_call | solution.py:194
  39.1 0.1 select_maximum_fusion.1
  39.2 0.1 select_maximum_fusion.couple_ref
  39.2 17.7 %all-to-all-done = bf16[64,32,128]{2,1,0:T(8,128)(2,1)} async-done(((bf16[64,32,128]{2,1,0:T(8,128)(2,1)}), bf16[64,32,128]{2,1,0:T(8,128)(2,1)}, u32[]{:S(2)}, u32[]{:S(2)}) %all-to-all-start) | async-done | bytes 524320 | tf_op jit(solution)/shard_map/all_to_all | solution.py:498
  56.9 3.1 %partial_sums.1 = bf16[3328,128]{1,0:T(8,128)(2,1)S(1)} custom-call(s32[10]{0:T(128)S(1)} %dynamic_slice.6.own_ref, bf16[10,640,192]{2,1,0:T(8,128)(2,1)S(1)} %get-tuple-element.20.turned_ref, bf16[2048,128]{1,0:T(8,128)(2,1)} %bitcast.7.got_ref), custom_call_target="tpu_custom_call" | custom-call | flops 314572800 | bytes 5000000 | tf_op jit(solution)/shard_map/partial_sums/pallas_call | solution.py:282
  60.0 18.2 %all_to_all.15.parts_ref = bf16[8,416,128]{2,1,0:T(8,128)(2,1)S(1)} all-to-all(bf16[8,416,128]{2,1,0:T(8,128)(2,1)S(1)} %bitcast.13), channel_id=1, replica_groups=mesh['lat'=8,'wave'=64] {'lat'}, dimensions={0} | all-to-all | bytes 1703936 | tf_op jit(solution)/shard_map/all_to_all | solution.py:510
  78.3 1.1 couple_levels.1
  79.3 13.6 %all_gather.3.all_ref = bf16[3328,128]{1,0:T(8,128)(2,1)S(1)} all-gather(bf16[416,128]{1,0:T(8,128)(2,1)S(1)} %couple_levels.1), channel_id=1, replica_groups=mesh['lat'=8,'wave'=64] {'lat'}, dimensions={0}, use_global_device_ids=true | all-gather | bytes 958464 | tf_op jit(solution)/shard_map/all_gather | solution.py:512
  92.9 4.1 %inverse_sums.1 = (bf16[10,80,128]{2,1,0:T(8,128)(2,1)}, bf16[2048,128]{1,0:T(8,128)(2,1)S(1)}) custom-call(s32[10]{0:T(128)S(1)} %dynamic_slice.6.own_ref, s32[1]{0:T(128)} %dynamic_slice.7.block_ref, bf16[10,192,640]{2,1,0:T(8,128)(2,1)S(1)} %copy-done.1, bf16[3328,128]{1,0:T(8,128)(2,1)S(1)} %all_gather.3.all_ref), custom_call_target="tpu_custom_call" | custom-call | flops 314572800 | bytes 5000000 | tf_op jit(solution)/shard_map/inverse_sums/pallas_call | solution.py:380
  97.0 38.9 %all_to_all.16 = bf16[64,32,128]{2,1,0:T(8,128)(2,1)S(1)} all-to-all(bf16[64,32,128]{2,1,0:T(8,128)(2,1)S(1)} %bitcast.15), channel_id=1, replica_groups=mesh['lat'=8,'wave'=64] {'wave'}, dimensions={0} | all-to-all | bytes 1048576 | tf_op jit(solution)/shard_map/all_to_all | solution.py:514
  135.9 4.0 %finish_rows.1 = bf16[192,2560]{1,0:T(8,128)(2,1)} custom-call(bf16[2048,128]{1,0:T(8,128)(2,1)S(1)} %bitcast.14, f32[1,640]{1,0:T(1,128)S(1)} %convert_element_type.34.sign_ref, bf16[2,640,1280]{2,1,0:T(8,128)(2,1)} %inverse_table.1.table_ref), custom_call_target="tpu_custom_call" | custom-call | flops 1258291200 | bytes 6000000 | tf_op jit(solution)/shard_map/finish_rows/pallas_call | solution.py:461
  (16 shorter events, 0.2 us)
Async XLA Ops:
  0.6 24.7 %copy-start.5 = (s32[640]{0:T(1024)S(1)}, s32[640]{0:T(1024)}, u32[]{:S(2)}) copy-start(s32[640]{0:T(1024)} %waves_ref.1) | copy-start | bytes 7684
  0.6 24.8 %copy-start.3 = (f32[32,32]{1,0:T(8,128)S(1)}, f32[32,32]{1,0:T(8,128)}, u32[]{:S(2)}) copy-start(f32[32,32]{1,0:T(8,128)} %param.10) | copy-start | bytes 12292
  0.7 24.8 %copy-start.4 = (f32[32,32]{1,0:T(8,128)S(1)}, f32[32,32]{1,0:T(8,128)}, u32[]{:S(2)}) copy-start(f32[32,32]{1,0:T(8,128)} %param.11) | copy-start | bytes 12292
  0.7 25.5 %copy-start.6 = (s32[8]{0:T(128)S(1)}, s32[8]{0:T(128)}, u32[]{:S(2)}) copy-start(s32[8]{0:T(128)} %param.9) | copy-start | bytes 100
  6.3 50.6 %all-to-all-start = ((bf16[64,32,128]{2,1,0:T(8,128)(2,1)}), bf16[64,32,128]{2,1,0:T(8,128)(2,1)}, u32[]{:S(2)}, u32[]{:S(2)}) async-start(bf16[64,32,128]{2,1,0:T(8,128)(2,1)} %bitcast.17), calls=%async_computation | async-start | bytes 1048576 | tf_op jit(solution)/shard_map/all_to_all | solution.py:498
  26.8 1.7 %copy-start.2 = (bf16[10,192,640]{2,1,0:T(8,128)(2,1)S(1)}, bf16[10,192,640]{2,1,0:T(8,128)(2,1)}, u32[]{:S(2)}) copy-start(bf16[10,192,640]{2,1,0:T(8,128)(2,1)} %leg_ref.1) | copy-start | bytes 7372804
  31.4 1.5 %copy-start = (bf16[10,192,640]{2,1,0:T(8,128)(2,1)}, bf16[10,192,640]{2,1,0:T(8,128)(2,1)S(1)}, u32[]{:S(2)}) copy-start(bf16[10,192,640]{2,1,0:T(8,128)(2,1)S(1)} %get-tuple-element.18.straight_ref) | copy-start | bytes 7372804
  56.9 36.0 %copy-start.1 = (bf16[10,192,640]{2,1,0:T(8,128)(2,1)S(1)}, bf16[10,192,640]{2,1,0:T(8,128)(2,1)}, u32[]{:S(2)}) copy-start(bf16[10,192,640]{2,1,0:T(8,128)(2,1)} %copy-done) | copy-start | bytes 7372804

commit v7 on v6

--- a/solution.py
+++ b/solution.py
@@ -29,7 +29,7 @@
 SHARE = PACKED // GROUPS
 VMEM_LIMIT = 24 * 1024 * 1024
 LARGE = 58 * 1024 * 1024
-MIDDLE = 52 * 1024 * 1024
+MIDDLE = 40 * 1024 * 1024
 
 
 def params(limit=VMEM_LIMIT):

time: 141 us -> 140 us (level)
    unnamed x16 -> x18, local copies, waits for them, and re-layouts: 3.32 us -> 3.32 us
where the time goes in v7:
time: 140 us; the launch traced here: 139 us
  blocking collectives  70.7 us (50%)
  Pallas kernels  25.6 us (18%)
  starting transfers between devices  19 us (14%)
  waiting for transfers between devices  17.7 us (13%)
  local copies, waits for them, and re-layouts  5.46 us (4%)
    all_to_all x1, blocking collectives, body(): got = swap(send.reshape(WAVES, CHUNK, K), 'wave')  38.9 us
    all_to_all x1, starting transfers between devices, body(): got = swap(send.reshape(WAVES, CHUNK, K), 'wave')  19 us
    all_to_all x1, blocking collectives, body(): parts = swap(packed.reshape(GROUPS, SHARE, K), 'lat')  18.2 us
    all_to_all x1, waiting for transfers between devices, body(): got = swap(send.reshape(WAVES, CHUNK, K), 'wave')  17.7 us
    all_gather x1, blocking collectives, body(): everything = lax.all_gather(spectral, 'lat', axis=0, tiled=True)  13.6 us
    pallas_call x1, Pallas kernels, forward(): pl.pallas_call(forward_kernel, grid=(TOP // 128,), in_specs=[pl.BlockSpec...  5.65 us
    pallas_call x1, Pallas kernels, inverse_table(): pl.pallas_call(table_kernel, grid=(5,), in_specs=[pl.BlockSpec((128, 128)...  5.32 us
    pallas_call x1, Pallas kernels, inverse(): pl.pallas_call(inverse_kernel, grid=(5,), in_specs=[pl.BlockSpec(memory_s...  4.05 us
  transfers between devices with their start and end apart: 1, of which 1 were waited for; matrix products, arithmetic and copies ran while one was open for 2% of the time, Pallas kernels for 6%

profile of v7, /device:TPU:6, one launch (start us, length us, event | category | flops | bytes accessed | tf_op | source)
XLA Modules:
  0.0 139.3 jit_solution(6762832414752766004)
XLA Ops:
  0.7 5.6 %forward_rows.1 = bf16[2048,128]{1,0:T(8,128)(2,1)} custom-call(s32[640]{0:T(1024)} %waves_ref.1, bf16[192,2560]{1,0:T(8,128)(2,1)} %bitcast.22), custom_call_target="tpu_custom_call" | custom-call | flops 1258291200 | bytes 2000000 | tf_op jit(solution)/shard_map/forward_rows/pallas_call | solution.py:152
  6.3 19.0 %all-to-all-start = ((bf16[64,32,128]{2,1,0:T(8,128)(2,1)}), bf16[64,32,128]{2,1,0:T(8,128)(2,1)}, u32[]{:S(2)}, u32[]{:S(2)}) async-start(bf16[64,32,128]{2,1,0:T(8,128)(2,1)} %bitcast.17), calls=%async_computation | async-start | bytes 1048576 | tf_op jit(solution)/shard_map/all_to_all | solution.py:498
  25.3 0.1 dynamic_slice.6.own_ref
  25.6 0.1 reshape.78
  25.7 0.1 copy.11
  25.8 0.1 convert_element_type.34.sign_ref
  25.9 0.1 convert_element_type.30
  26.0 0.1 copy.10
  26.2 0.6 dynamic_slice.7.block_ref
  26.8 1.7 %copy-done.3 = bf16[10,192,640]{2,1,0:T(8,128)(2,1)S(1)} copy-done((bf16[10,192,640]{2,1,0:T(8,128)(2,1)S(1)}, bf16[10,192,640]{2,1,0:T(8,128)(2,1)}, u32[]{:S(2)}) %copy-start.3) | copy-done | bytes 2457624
  28.5 2.9 %basis_rows.1 = (bf16[10,192,640]{2,1,0:T(8,128)(2,1)S(1)}, bf16[10,640,192]{2,1,0:T(8,128)(2,1)S(1)}) custom-call(s32[10]{0:T(128)S(1)} %dynamic_slice.6.own_ref, bf16[10,192,640]{2,1,0:T(8,128)(2,1)S(1)} %copy-done.3), custom_call_target="tpu_custom_call" | custom-call | bytes 30000000 | tf_op jit(solution)/shard_map/basis_rows/pallas_call | solution.py:223
  31.4 1.5 %copy-done.1 = bf16[10,192,640]{2,1,0:T(8,128)(2,1)} copy-done((bf16[10,192,640]{2,1,0:T(8,128)(2,1)}, bf16[10,192,640]{2,1,0:T(8,128)(2,1)S(1)}, u32[]{:S(2)}) %copy-start.1) | copy-done | bytes 2457624
  32.9 0.9 broadcast_in_dim.2.waves_ref
  33.7 5.3 %inverse_table.1.table_ref = bf16[2,640,1280]{2,1,0:T(8,128)(2,1)} custom-call(f32[640,128]{1,0:T(8,128)} %broadcast_in_dim.2.waves_ref), custom_call_target="tpu_custom_call" | custom-call | flops 30000000 | bytes 6000000 | tf_op jit(solution)/shard_map/inverse_table/pallas_call | solution.py:194
  39.1 0.1 select_maximum_fusion.1
  39.1 0.1 select_maximum_fusion.couple_ref
  39.2 17.7 %all-to-all-done = bf16[64,32,128]{2,1,0:T(8,128)(2,1)} async-done(((bf16[64,32,128]{2,1,0:T(8,128)(2,1)}), bf16[64,32,128]{2,1,0:T(8,128)(2,1)}, u32[]{:S(2)}, u32[]{:S(2)}) %all-to-all-start) | async-done | bytes 524320 | tf_op jit(solution)/shard_map/all_to_all | solution.py:498
  56.9 3.1 %partial_sums.1 = bf16[3328,128]{1,0:T(8,128)(2,1)S(1)} custom-call(s32[10]{0:T(128)S(1)} %dynamic_slice.6.own_ref, bf16[10,640,192]{2,1,0:T(8,128)(2,1)S(1)} %get-tuple-element.20.turned_ref, bf16[2048,128]{1,0:T(8,128)(2,1)} %bitcast.7.got_ref), custom_call_target="tpu_custom_call" | custom-call | flops 314572800 | bytes 5000000 | tf_op jit(solution)/shard_map/partial_sums/pallas_call | solution.py:282
  60.0 18.2 %all_to_all.15.parts_ref = bf16[8,416,128]{2,1,0:T(8,128)(2,1)S(1)} all-to-all(bf16[8,416,128]{2,1,0:T(8,128)(2,1)S(1)} %bitcast.13), channel_id=1, replica_groups=mesh['lat'=8,'wave'=64] {'lat'}, dimensions={0} | all-to-all | bytes 1703936 | tf_op jit(solution)/shard_map/all_to_all | solution.py:510
  78.3 1.1 couple_levels.1
  79.3 13.6 %all_gather.3.all_ref = bf16[3328,128]{1,0:T(8,128)(2,1)S(1)} all-gather(bf16[416,128]{1,0:T(8,128)(2,1)S(1)} %couple_levels.1), channel_id=1, replica_groups=mesh['lat'=8,'wave'=64] {'lat'}, dimensions={0}, use_global_device_ids=true | all-gather | bytes 958464 | tf_op jit(solution)/shard_map/all_gather | solution.py:512
  92.9 4.0 %inverse_sums.1 = (bf16[10,80,128]{2,1,0:T(8,128)(2,1)}, bf16[2048,128]{1,0:T(8,128)(2,1)S(1)}) custom-call(s32[10]{0:T(128)S(1)} %dynamic_slice.6.own_ref, s32[1]{0:T(128)} %dynamic_slice.7.block_ref, bf16[10,192,640]{2,1,0:T(8,128)(2,1)S(1)} %copy-done.2, bf16[3328,128]{1,0:T(8,128)(2,1)S(1)} %all_gather.3.all_ref), custom_call_target="tpu_custom_call" | custom-call | flops 314572800 | bytes 5000000 | tf_op jit(solution)/shard_map/inverse_sums/pallas_call | solution.py:380
  97.0 38.9 %all_to_all.16 = bf16[64,32,128]{2,1,0:T(8,128)(2,1)S(1)} all-to-all(bf16[64,32,128]{2,1,0:T(8,128)(2,1)S(1)} %bitcast.15), channel_id=1, replica_groups=mesh['lat'=8,'wave'=64] {'wave'}, dimensions={0} | all-to-all | bytes 1048576 | tf_op jit(solution)/shard_map/all_to_all | solution.py:514
  135.9 3.4 %finish_rows.1 = bf16[192,2560]{1,0:T(8,128)(2,1)} custom-call(bf16[2048,128]{1,0:T(8,128)(2,1)S(1)} %bitcast.14, f32[1,640]{1,0:T(1,128)S(1)} %convert_element_type.34.sign_ref, bf16[2,640,1280]{2,1,0:T(8,128)(2,1)S(1)} %copy-done), custom_call_target="tpu_custom_call" | custom-call | flops 1258291200 | bytes 6000000 | tf_op jit(solution)/shard_map/finish_rows/pallas_call | solution.py:461
  (18 shorter events, 0.2 us)
Async XLA Ops:
  0.6 24.7 %copy-start.6 = (s32[640]{0:T(1024)S(1)}, s32[640]{0:T(1024)}, u32[]{:S(2)}) copy-start(s32[640]{0:T(1024)} %waves_ref.1) | copy-start | bytes 7684
  0.6 24.8 %copy-start.4 = (f32[32,32]{1,0:T(8,128)S(1)}, f32[32,32]{1,0:T(8,128)}, u32[]{:S(2)}) copy-start(f32[32,32]{1,0:T(8,128)} %param.10) | copy-start | bytes 12292
  0.7 24.8 %copy-start.5 = (f32[32,32]{1,0:T(8,128)S(1)}, f32[32,32]{1,0:T(8,128)}, u32[]{:S(2)}) copy-start(f32[32,32]{1,0:T(8,128)} %param.11) | copy-start | bytes 12292
  0.7 25.5 %copy-start.7 = (s32[8]{0:T(128)S(1)}, s32[8]{0:T(128)}, u32[]{:S(2)}) copy-start(s32[8]{0:T(128)} %param.9) | copy-start | bytes 100
  6.3 50.6 %all-to-all-start = ((bf16[64,32,128]{2,1,0:T(8,128)(2,1)}), bf16[64,32,128]{2,1,0:T(8,128)(2,1)}, u32[]{:S(2)}, u32[]{:S(2)}) async-start(bf16[64,32,128]{2,1,0:T(8,128)(2,1)} %bitcast.17), calls=%async_computation | async-start | bytes 1048576 | tf_op jit(solution)/shard_map/all_to_all | solution.py:498
  26.8 1.7 %copy-start.3 = (bf16[10,192,640]{2,1,0:T(8,128)(2,1)S(1)}, bf16[10,192,640]{2,1,0:T(8,128)(2,1)}, u32[]{:S(2)}) copy-start(bf16[10,192,640]{2,1,0:T(8,128)(2,1)} %leg_ref.1) | copy-start | bytes 7372804
  31.4 1.5 %copy-start.1 = (bf16[10,192,640]{2,1,0:T(8,128)(2,1)}, bf16[10,192,640]{2,1,0:T(8,128)(2,1)S(1)}, u32[]{:S(2)}) copy-start(bf16[10,192,640]{2,1,0:T(8,128)(2,1)S(1)} %get-tuple-element.18.straight_ref) | copy-start | bytes 7372804
  56.9 36.0 %copy-start.2 = (bf16[10,192,640]{2,1,0:T(8,128)(2,1)S(1)}, bf16[10,192,640]{2,1,0:T(8,128)(2,1)}, u32[]{:S(2)}) copy-start(bf16[10,192,640]{2,1,0:T(8,128)(2,1)} %copy-done.1) | copy-start | bytes 7372804
  78.3 57.7 %copy-start = (bf16[2,640,1280]{2,1,0:T(8,128)(2,1)S(1)}, bf16[2,640,1280]{2,1,0:T(8,128)(2,1)}, u32[]{:S(2)}) copy-start(bf16[2,640,1280]{2,1,0:T(8,128)(2,1)} %inverse_table.1.table_ref) | copy-start | bytes 9830404
